TPU v7x, 256 devices: a whole 4x4x8 slice. The times are simulated.
256 devices in a mesh: cfg: 2 (over core), uly: 4 (over y), blk: 32 (over x, z).
Axes of the slice: x: 4, y: 4, z: 8, core: 2. Of those that a mesh axis runs over, the one named last changes fastest.
Arguments:
- residual_in: bfloat16 [2, 8192, 5120], P('cfg', ('uly', 'blk')), may hold values from -1.1953125 to 1.1953125
- projected: bfloat16 [2, 8192, 7680], P('cfg', ('uly', 'blk')), may hold values from -1500 to 1500, as said below
- query_gain: float32 [2560], replicated, may hold values from 0.6 to 5
- key_gain: float32 [2560], replicated, may hold values from 0.6 to 5
- gate_scale: float32 [5120], replicated, may hold values from -3 to 3
- out_weight: bfloat16 [2560, 5120], P('uly'), may hold values from -0.125 to 0.125
- out_bias: float32 [5120], replicated, may hold values from -3 to 3
Outputs:
- pass_outputs: bfloat16 [2, 8192, 5120], P(None, ('uly', 'blk'), 'cfg')
Inputs may be any that keep to these rules, and one draw needn't show every extreme that they name: `projected`: query and key features carry token scales and feature scales; value features are of order one.
All inputs are finite; a program needn't handle non-finite values.
Results may differ from a plain program's by a relative error of at most 0.015.
Values may be sent and summed in bfloat16 or wider, within the bound.
No kernel may reach another device: no remote copies, remote signals or barrier semaphores. Data moves between devices by JAX's collectives and lax.ppermute only.
A program may use at most 192 MiB of HBM per device.

v0:
```python
import math

import jax
import jax.numpy as jnp
import numpy as np
from jax import lax
from jax.experimental import pallas as pl
from jax.experimental.pallas import tpu as pltpu
from jax.sharding import Mesh
from jax.sharding import PartitionSpec as P

D = 5120
HEADS = 20
HEAD = 128
GH = 30
GW = 52
ULY = 4
XS = 4
ZS = 8
ROWS = 64
GROUP = 5
GF = GROUP * HEAD
FEAT = HEADS * HEAD
HALF = D // 2
QUART = HALF // 2
OH = GF + 16
BF = jnp.bfloat16
F32 = jnp.float32
SCALE = math.log2(math.e) / math.sqrt(HEAD)
VMEM = 48 * 1024 * 1024


def params(limit=VMEM):
    return pltpu.CompilerParams(vmem_limit_bytes=limit)


def swap_uly(a, s):
    return lax.ppermute(a, "uly", [(i, i ^ s) for i in range(ULY)])


def swap_x(a, s):
    return lax.ppermute(a, "x", [(i, i ^ s) for i in range(XS)])


def swap_z(a, odd):
    return lax.ppermute(a, "z", [(i, ((i - odd ^ 1) + odd) % ZS) for i in range(ZS)])


def swap_cfg(a):
    return lax.ppermute(a, "cfg", [(0, 1), (1, 0)])


FRAME = HEAD - 4 * (HEAD // 6)
SPACE = 2 * (HEAD // 6)


def rates():
    def freq(extent):
        return 1.0 / 10000.0 ** (np.arange(0, extent, 2, dtype=np.float32) / np.float32(extent))

    each = np.concatenate([freq(FRAME), freq(SPACE), freq(SPACE)]).astype(np.float32)
    return np.repeat(each, 2)[None]


def tables(first, rate):
    pos = first + lax.broadcasted_iota(jnp.int32, (ROWS, HEAD), 0)
    lane = lax.broadcasted_iota(jnp.int32, (ROWS, HEAD), 1)
    where = jnp.where(
        lane < FRAME, pos // (GH * GW), jnp.where(lane < FRAME + SPACE, pos // GW % GH, pos % GW)
    ).astype(F32)
    angle = where * rate
    sine = jnp.sin(angle)
    even = lane % 2 == 0
    return jnp.cos(angle), jnp.where(even, -sine, 0.0), jnp.where(even, 0.0, sine)


BLOCK = 3 * ROWS


def prep_body(at_ref, proj_ref, q_gain, k_gain, rate_ref, *outs):
    u = at_ref[0]
    cosine, s_even, s_odd = tables(at_ref[1], rate_ref[...])
    gains = (q_gain, k_gain)

    def scale_of(base):
        total = jnp.zeros((ROWS, HEAD), F32)
        for h in range(HEADS):
            part = proj_ref[0, :, base + h * HEAD : base + (h + 1) * HEAD].astype(F32)
            total = total + part * part
        return lax.rsqrt(jnp.sum(total, axis=1, keepdims=True) * (1.0 / FEAT) + 1e-06)

    scales = (scale_of(0), scale_of(FEAT))

    def turned(which, at):
        x = proj_ref[0, :, pl.ds(pl.multiple_of(which * FEAT + at, HEAD), HEAD)].astype(F32)
        x = x * scales[which] * gains[which][pl.ds(at, HEAD)][None]
        x = x * cosine + pltpu.roll(x, HEAD - 1, 1) * s_even + pltpu.roll(x, 1, 1) * s_odd
        return x.astype(BF)

    for s in range(ULY):
        start = (u ^ s) * GF
        for h in range(GROUP):
            here = slice(h * HEAD, (h + 1) * HEAD)
            at = pl.multiple_of(start + h * HEAD, HEAD)
            outs[s][0:ROWS, here] = turned(1, at)
            outs[s][2 * ROWS :, here] = turned(0, at)
        outs[s][ROWS : 2 * ROWS, :] = proj_ref[
            0, :, pl.ds(pl.multiple_of(2 * FEAT + start, HEAD), GF)
        ]


def prep(place, projected, query_gain, key_gain):
    def whole(shape):
        return pl.BlockSpec(shape, lambda i: (0,) * len(shape))

    rate = jnp.asarray(rates())
    args = (projected, query_gain, key_gain, rate)
    return pl.pallas_call(
        prep_body,
        grid=(1,),
        in_specs=[pl.BlockSpec(memory_space=pltpu.SMEM)] + [whole(a.shape) for a in args],
        out_specs=[whole((BLOCK, GF))] * ULY,
        out_shape=[jax.ShapeDtypeStruct((BLOCK, GF), BF)] * ULY,
        compiler_params=params(62 * 1024 * 1024),
        name="prep",
    )(place, *args)


QB = 256


def heads_step(q, kvs, h, m_old):
    here = slice(h * HEAD, (h + 1) * HEAD)
    keys = jnp.concatenate([kv[0 : kv.shape[0] // 2, here] for kv in kvs], axis=0)
    vals = jnp.concatenate([kv[kv.shape[0] // 2 :, here] for kv in kvs], axis=0)
    s = lax.dot_general(keys, q[:, here], (((1,), (1,)), ((), ())), preferred_element_type=F32)
    m = jnp.max(s, axis=0, keepdims=True) * SCALE
    if m_old is not None:
        m = jnp.maximum(m, m_old)
    e = jnp.exp2(s * SCALE - m).astype(BF)
    both = jnp.concatenate([vals, jnp.ones_like(vals)], axis=1)
    o = lax.dot_general(both, e, (((0,), (0,)), ((), ())), preferred_element_type=F32)
    return m, o[HEAD : HEAD + 1], o[:HEAD]


def attend_body(n_kv, first, *refs):
    q_ref = refs[0]
    kv_refs = refs[1 : 1 + n_kv]
    if first:
        acc_out, ml_out = refs[1 + n_kv :]
    else:
        acc_in, ml_in, acc_out, ml_out = refs[1 + n_kv :]
    tops = []
    sums = []
    for h in range(GROUP):
        m_old = None if first else ml_in[h : h + 1, :]
        m, l, o = heads_step(q_ref, kv_refs, h, m_old)
        here = slice(h * HEAD, (h + 1) * HEAD)
        if not first:
            alpha = jnp.exp2(m_old - m)
            l = l + alpha * ml_in[8 + h : 9 + h, :]
            o = o + alpha * acc_in[here, :]
        acc_out[here, :] = o
        tops.append(m)
        sums.append(l)
    blank = jnp.zeros((8 - GROUP, QB), F32)
    ml_out[...] = jnp.concatenate([*tops, blank, *sums, blank], axis=0)


def attend(q, kvs, state=None):
    rows = q.shape[0]
    n_keys = sum(kv.shape[0] // 2 for kv in kvs)

    def col(i):
        return (0, i)

    specs = [pl.BlockSpec((QB, GF), lambda i: (i, 0))]
    specs += [pl.BlockSpec(kv.shape, lambda i: (0, 0)) for kv in kvs]
    args = [q, *kvs]
    acc_spec = pl.BlockSpec((GF, QB), col)
    ml_spec = pl.BlockSpec((16, QB), col)
    aliases = {}
    if state is not None:
        aliases = {len(args): 0, len(args) + 1: 1}
        specs += [acc_spec, ml_spec]
        args += list(state)
    return pl.pallas_call(
        lambda *r: attend_body(len(kvs), state is None, *r),
        grid=(rows // QB,),
        in_specs=specs,
        out_specs=[acc_spec, ml_spec],
        out_shape=[
            jax.ShapeDtypeStruct((GF, rows), F32),
            jax.ShapeDtypeStruct((16, rows), F32),
        ],
        input_output_aliases=aliases,
        compiler_params=params(),
        cost_estimate=pl.CostEstimate(
            flops=4 * rows * n_keys * GF,
            transcendentals=rows * n_keys * GROUP,
            bytes_accessed=rows * GF * 10,
        ),
        name="attend",
    )(*args)


def attend_last_body(n_kv, n_out, *refs):
    q_ref = refs[0]
    kv_refs = refs[1 : 1 + n_kv]
    acc_in, ml_in = refs[1 + n_kv : 3 + n_kv]
    outs = refs[3 + n_kv :]
    his, mids, lows = [], [], []
    parts = []
    for h in range(GROUP):
        m_old = ml_in[h : h + 1, :]
        m, l, o = heads_step(q_ref, kv_refs, h, m_old)
        here = slice(h * HEAD, (h + 1) * HEAD)
        alpha = jnp.exp2(m_old - m)
        l = l + alpha * ml_in[8 + h : 9 + h, :]
        o = o + alpha * acc_in[here, :]
        parts.append((o / l).astype(BF))
        lse = m + jnp.log2(l)
        hi = lse.astype(BF).astype(F32)
        mid = (lse - hi).astype(BF).astype(F32)
        his.append(hi)
        mids.append(mid)
        lows.append(lse - hi - mid)
    stats = jnp.concatenate([*his, *mids, *lows, jnp.zeros((1, QB), F32)], axis=0).astype(BF)
    for i in range(n_out):

        @pl.when(pl.program_id(0) == i)
        def _(i=i):
            for h in range(GROUP):
                outs[i][h * HEAD : (h + 1) * HEAD, :] = parts[h]
            outs[i][GF:, :] = stats


def attend_last(q, kvs, state, blocks):
    def place(i):
        back = blocks[0]
        for n, r in enumerate(blocks[1:], 1):
            back = jnp.where(i == n, r, back)
        return back

    n = len(blocks)
    n_keys = sum(kv.shape[0] // 2 for kv in kvs)
    specs = [pl.BlockSpec((QB, GF), lambda i: (place(i), 0))]
    specs += [pl.BlockSpec(kv.shape, lambda i: (0, 0)) for kv in kvs]
    specs += [
        pl.BlockSpec((GF, QB), lambda i: (0, place(i))),
        pl.BlockSpec((16, QB), lambda i: (0, place(i))),
    ]
    return pl.pallas_call(
        lambda *r: attend_last_body(len(kvs), n, *r),
        grid=(n,),
        in_specs=specs,
        out_specs=[pl.BlockSpec((OH, QB), lambda i: (0, 0))] * n,
        out_shape=[jax.ShapeDtypeStruct((OH, QB), BF)] * n,
        compiler_params=params(),
        cost_estimate=pl.CostEstimate(
            flops=4 * n * QB * n_keys * GF,
            transcendentals=n * QB * n_keys * GROUP,
            bytes_accessed=n * QB * GF * 8,
        ),
        name="attend_last",
    )(q, *kvs, *state)


def join_body(*refs):
    parts, out_ref = refs[:-1], refs[-1]
    tails = [p[GF:, :].astype(F32) for p in parts]
    for h in range(GROUP):
        here = slice(h * HEAD, (h + 1) * HEAD)
        lse = [t[h : h + 1] + t[GROUP + h : GROUP + h + 1] + t[2 * GROUP + h : 2 * GROUP + h + 1] for t in tails]
        top = lse[0]
        for other in lse[1:]:
            top = jnp.maximum(top, other)
        weights = [jnp.exp2(v - top) for v in lse]
        total = weights[0]
        for other in weights[1:]:
            total = total + other
        o = weights[0] * parts[0][here, :].astype(F32)
        for w, p in zip(weights[1:], parts[1:]):
            o = o + w * p[here, :].astype(F32)
        out_ref[:, here] = (o / total).T.astype(BF)


def join(parts):
    return pl.pallas_call(
        join_body,
        grid=(2,),
        in_specs=[pl.BlockSpec((OH, QB // 2), lambda i: (0, i))] * len(parts),
        out_specs=pl.BlockSpec((QB // 2, GF), lambda i: (i, 0)),
        out_shape=jax.ShapeDtypeStruct((QB, GF), BF),
        compiler_params=params(),
        name="join",
    )(*parts)


def project_body(blocks, c_ref, own_ref, other_ref, w_ref, *outs):
    lhs = jnp.concatenate(
        [ref[s * ROWS : (s + 1) * ROWS] for s in blocks for ref in (own_ref, other_ref)], axis=0
    )
    y = jnp.dot(lhs, w_ref[...], preferred_element_type=F32).astype(BF)
    for half in range(2):

        @pl.when(pl.program_id(0) == half)
        def _(half=half):
            for i in range(len(blocks)):
                outs[2 * i + half][...] = y[2 * ROWS * i : 2 * ROWS * (i + 1)]


def project(c, own, other, weight, blocks):
    n = 2 * len(blocks)
    grid_spec = pltpu.PrefetchScalarGridSpec(
        num_scalar_prefetch=1,
        grid=(2,),
        in_specs=[
            pl.BlockSpec((QB, GF), lambda i, c_ref: (0, 0)),
            pl.BlockSpec((QB, GF), lambda i, c_ref: (0, 0)),
            pl.BlockSpec((GF, QUART), lambda i, c_ref: (0, c_ref[0] * 2 + i)),
        ],
        out_specs=[pl.BlockSpec((2 * ROWS, QUART), lambda i, c_ref: (0, 0))] * n,
    )
    return pl.pallas_call(
        lambda *r: project_body(blocks, *r),
        grid_spec=grid_spec,
        out_shape=[jax.ShapeDtypeStruct((2 * ROWS, QUART), BF)] * n,
        compiler_params=params(),
        name="project",
    )(c, own, other, weight)


def finish_body(c_ref, own_ref, other_ref, gate_ref, bias_ref, *refs):
    out_ref = refs[-1]
    c = c_ref[0]

    def write(parts):
        mixed = parts[0][...].astype(F32)
        for ref in parts[1:]:
            mixed = mixed + ref[...].astype(F32)
        at = pl.ds(pl.multiple_of((2 * c + pl.program_id(0)) * QUART, HEAD), QUART)
        branch = gate_ref[at][None] * (mixed + bias_ref[at][None])
        out_ref[c] = (own_ref[0].astype(F32) + branch[0:ROWS]).astype(BF)
        out_ref[1 - c] = (other_ref[...].astype(F32) + branch[ROWS:]).astype(BF)

    for half in range(2):

        @pl.when(pl.program_id(0) == half)
        def _(half=half):
            write(refs[half:6:2])


def finish(c, residual, other, gate, bias, parts):
    piece = pl.BlockSpec((2 * ROWS, QUART), lambda i, c_ref: (0, 0))
    line = pl.BlockSpec((D,), lambda i, c_ref: (0,))
    grid_spec = pltpu.PrefetchScalarGridSpec(
        num_scalar_prefetch=1,
        grid=(2,),
        in_specs=[
            pl.BlockSpec((1, ROWS, QUART), lambda i, c_ref: (0, 0, 2 * c_ref[0] + i)),
            pl.BlockSpec((ROWS, QUART), lambda i, c_ref: (0, i)),
            line,
            line,
        ]
        + [piece] * 6,
        out_specs=pl.BlockSpec((2, ROWS, QUART), lambda i, c_ref: (0, 0, i)),
    )
    return pl.pallas_call(
        finish_body,
        grid_spec=grid_spec,
        out_shape=jax.ShapeDtypeStruct((2, ROWS, HALF), BF),
        compiler_params=params(),
        name="finish",
    )(c, residual, other, gate, bias, *parts)


def add(a, b):
    return (a.astype(F32) + b.astype(F32)).astype(BF)


def after(values, *earlier):
    tied = lax.optimization_barrier((tuple(values), earlier))
    return list(tied[0])


def on_device(residual_in, projected, query_gain, key_gain, gate_scale, out_weight, out_bias):
    u = lax.axis_index("uly")
    x = lax.axis_index("x")
    c_arr = lax.axis_index("cfg").astype(jnp.int32)[None]
    first = ((u * XS + x) * ZS + lax.axis_index("z")) * ROWS
    place = jnp.stack([u, first]).astype(jnp.int32)
    sent = prep(place, projected, query_gain, key_gain)

    far = swap_uly(sent[2], 2)
    got = [sent[0], swap_uly(sent[1], 1), far, swap_uly(sent[3], 3)]
    own = jnp.concatenate([a[:ROWS] for a in got] + [a[ROWS : 2 * ROWS] for a in got], axis=0)
    q_own = jnp.concatenate([a[2 * ROWS :] for a in got], axis=0)

    left, right = swap_z(own, 0), swap_z(own, 1)

    (q_sent,) = after([q_own], left)
    q_far = swap_x(q_sent, 2)
    q_all = jnp.concatenate([q_own, swap_x(q_sent, 1), q_far, swap_x(q_sent, 3)], axis=0)

    left2, right2 = swap_z(right, 0), swap_z(left, 1)
    left3, right3 = swap_z(right2, 0), swap_z(left2, 1)
    state = attend(q_all, [own])
    state = attend(q_all, [left, right], state)
    state = attend(q_all, [left2, right2], state)
    left3, right3 = after([left3, right3], *state)
    half = own.shape[0] // 2
    top = jnp.concatenate([right3[: half // 2], right3[half : half + half // 2]], axis=0)
    low = jnp.concatenate([left3[half // 2 : half], left3[half + half // 2 :]], axis=0)
    kvs = [swap_z(top, 0), swap_z(low, 1)]
    state = attend(q_all, [left3, right3], state)

    (p2,) = attend_last(q_all, kvs, state, (2,))
    r2 = swap_x(p2, 2)
    (kv_a,) = after([kvs[0]], p2)
    p1, p3 = attend_last(q_all, [kv_a, kvs[1]], state, (1, 3))
    r1, r3 = swap_x(p1, 1), swap_x(p3, 3)
    (kv_b,) = after([kvs[0]], p1)
    (p0,) = attend_last(q_all, [kv_b, kvs[1]], state, (0,))
    mine = join([p0, r1, r2, r3])
    heads = (mine, swap_cfg(mine))

    p2a, p2b, p1a, p1b, p3a, p3b, p0a, p0b = project(c_arr, *heads, out_weight, (2, 1, 3, 0))
    via_one = swap_uly(p2a, 1)
    via_three = swap_uly(p2b, 3)
    residual_sent = lax.dynamic_slice(residual_in, (0, 0, (1 - c_arr[0]) * HALF), (1, ROWS, HALF))[0]
    (residual_sent,) = after([residual_sent], p1a)
    residual_other = swap_cfg(residual_sent)
    three_b = swap_uly(p3b, 3)
    one_a = swap_uly(p1a, 1)
    three_a = swap_uly(add(p3a, via_one), 3)
    one_b = swap_uly(add(p1b, via_three), 1)
    return finish(
        c_arr,
        residual_in,
        residual_other,
        gate_scale,
        out_bias,
        [p0a, p0b, three_a, three_b, one_a, one_b],
    )


def solution(mesh):
    fine = Mesh(mesh.devices.reshape(2, ULY, XS, ZS), ("cfg", "uly", "x", "z"))
    tokens = ("uly", "x", "z")
    in_specs = (
        P("cfg", tokens, None),
        P("cfg", tokens, None),
        P(),
        P(),
        P(),
        P("uly", None),
        P(),
    )
    out_specs = P(None, tokens, "cfg")
    return jax.shard_map(
        on_device, mesh=fine, in_specs=in_specs, out_specs=out_specs, check_vma=False
    )
```

profile of v0, /device:TPU:1, one launch (start us, length us, event | category | flops | bytes accessed | tf_op | source)
XLA Modules:
  0.0 138.5 jit_solution(862954893512876554)
XLA Ops:
  0.0 0.7 pad_add_fusion.at_ref
  0.7 3.0 %prep.1 = (bf16[192,640]{1,0:T(8,128)(2,1)}, bf16[192,640]{1,0:T(8,128)(2,1)}, bf16[192,640]{1,0:T(8,128)(2,1)}, bf16[192,640]{1,0:T(8,128)(2,1)}) custom-call(s32[2]{0:T(128)} %pad_add_fusion.at_ref, bf16[1,64,7680]{2,1,0:T(8,128)(2,1)} %proj_ref.1, f32[2560]{0:T(1024)} %q_gain.1, f32[2560]{0:T(1024)} %k_gain.1, f32[1,128]{1,0:T(1,128)} %constant.33.clone.rate_ref), custom_call_target="tpu_custom_call" | custom-call | tf_op jit(solution)/shard_map/prep/pallas_call | solution.py:118
  3.7 2.1 %collective-permute-start = (bf16[192,640]{1,0:T(8,128)(2,1)}, bf16[192,640]{1,0:T(8,128)(2,1)S(1)}, u32[]{:S(2)}, u32[]{:S(2)}) collective-permute-start(bf16[192,640]{1,0:T(8,128)(2,1)} %get-tuple-element.34), channel_id=1, source_target_pairs={{0,32},{32,0},{64,96},{96,64},{1,33},{33,1},{65,97},{97,65},{2,34}... | collective-permute-start | bytes 737288 | tf_op jit(solution)/shard_map/ppermute | solution.py:38
  5.8 2.6 %collective-permute-start.1 = (bf16[192,640]{1,0:T(8,128)(2,1)}, bf16[192,640]{1,0:T(8,128)(2,1)S(1)}, u32[]{:S(2)}, u32[]{:S(2)}) collective-permute-start(bf16[192,640]{1,0:T(8,128)(2,1)} %get-tuple-element.35), channel_id=1, source_target_pairs={{0,64},{32,96},{64,0},{96,32},{1,65},{33,97},{65,1},{97,33},{2,66}... | collective-permute-start | bytes 737288 | tf_op jit(solution)/shard_map/ppermute | solution.py:38
  8.4 0.0 collective-permute-start.2
  8.4 0.9 slice_dynamic-update-slice_fusion.7
  9.3 1.2 collective-permute-done
  10.5 8.7 %collective-permute-done.1 = bf16[192,640]{1,0:T(8,128)(2,1)S(1)} collective-permute-done((bf16[192,640]{1,0:T(8,128)(2,1)}, bf16[192,640]{1,0:T(8,128)(2,1)S(1)}, u32[]{:S(2)}, u32[]{:S(2)}) %collective-permute-start.1) | collective-permute-done | bytes 245792 | tf_op jit(solution)/shard_map/ppermute | solution.py:38
  19.3 2.1 %collective-permute-done.2 = bf16[192,640]{1,0:T(8,128)(2,1)S(1)} collective-permute-done((bf16[192,640]{1,0:T(8,128)(2,1)}, bf16[192,640]{1,0:T(8,128)(2,1)S(1)}, u32[]{:S(2)}, u32[]{:S(2)}) %collective-permute-start.2) | collective-permute-done | bytes 245792 | tf_op jit(solution)/shard_map/ppermute | solution.py:38
  21.4 1.0 slice_dynamic-update-slice_fusion.6
  22.5 5.7 %collective-permute-start.9 = (bf16[512,640]{1,0:T(8,128)(2,1)S(1)}, bf16[512,640]{1,0:T(8,128)(2,1)S(1)}, u32[]{:S(2)}, u32[]{:S(2)}) collective-permute-start(bf16[512,640]{1,0:T(8,128)(2,1)S(1)} %get-tuple-element.65.r_1_), channel_id=1, source_target_pairs={{0,7},{1,2},{2,1},{3,4},{4,3},{5,6},{6,5},{7,0},{8,15},{9,10},{10,... | collective-permute-start | bytes 1966088 | tf_op jit(solution)/shard_map/ppermute | solution.py:46
  28.2 0.0 collective-permute-start.3
  28.2 13.0 %collective-permute-done.9.r_2_ = bf16[512,640]{1,0:T(8,128)(2,1)S(1)} collective-permute-done((bf16[512,640]{1,0:T(8,128)(2,1)S(1)}, bf16[512,640]{1,0:T(8,128)(2,1)S(1)}, u32[]{:S(2)}, u32[]{:S(2)}) %collective-permute-start.9) | collective-permute-done | bytes 655392 | tf_op jit(solution)/shard_map/ppermute | solution.py:46
  41.2 0.0 collective-permute-start.10
  41.2 0.9 collective-permute-done.3.r_1_
  42.1 1.5 %collective-permute-start.7 = (bf16[512,640]{1,0:T(8,128)(2,1)S(1)}, bf16[512,640]{1,0:T(8,128)(2,1)S(1)}, u32[]{:S(2)}, u32[]{:S(2)}) collective-permute-start(bf16[512,640]{1,0:T(8,128)(2,1)S(1)} %collective-permute-done.3.r_1_), channel_id=1, source_target_pairs={{0,7},{1,2},{2,1},{3,4},{4,3},{5,6},{6,5},{7,0},{8,15},{9,10},{10,... | collective-permute-start | bytes 1966088 | tf_op jit(solution)/shard_map/ppermute | solution.py:46
  43.6 1.3 collective-permute-start.4
  44.9 2.5 %collective-permute-start.5 = (bf16[256,640]{1,0:T(8,128)(2,1)S(1)}, bf16[256,640]{1,0:T(8,128)(2,1)S(1)}, u32[]{:S(2)}, u32[]{:S(2)}) collective-permute-start(bf16[256,640]{1,0:T(8,128)(2,1)S(1)} %pad_maximum_fusion), channel_id=1, source_target_pairs={{0,16},{8,24},{16,0},{24,8},{1,17},{9,25},{17,1},{25,9},{2,18},{10... | collective-permute-start | bytes 983048 | tf_op jit(solution)/shard_map/ppermute | solution.py:42
  47.4 0.2 collective-permute-start.6
  47.6 9.2 %collective-permute-done.10.r_1_ = bf16[512,640]{1,0:T(8,128)(2,1)S(1)} collective-permute-done((bf16[512,640]{1,0:T(8,128)(2,1)S(1)}, bf16[512,640]{1,0:T(8,128)(2,1)S(1)}, u32[]{:S(2)}, u32[]{:S(2)}) %collective-permute-start.10) | collective-permute-done | bytes 655392 | tf_op jit(solution)/shard_map/ppermute | solution.py:46
  56.8 0.1 collective-permute-start.11
  56.8 0.0 collective-permute-done.7.r_2_
  56.9 0.9 collective-permute-start.8
  57.8 0.0 collective-permute-done.4
  57.8 0.8 collective-permute-done.5
  58.6 4.2 %collective-permute-done.6 = bf16[256,640]{1,0:T(8,128)(2,1)S(1)} collective-permute-done((bf16[256,640]{1,0:T(8,128)(2,1)S(1)}, bf16[256,640]{1,0:T(8,128)(2,1)S(1)}, u32[]{:S(2)}, u32[]{:S(2)}) %collective-permute-start.6) | collective-permute-done | bytes 327712 | tf_op jit(solution)/shard_map/ppermute | solution.py:42
  62.9 3.2 %attend.4 = (f32[640,1024]{1,0:T(8,128)S(1)}, f32[16,1024]{1,0:T(8,128)S(1)}) custom-call(bf16[1024,640]{1,0:T(8,128)(2,1)S(1)} %constant_dynamic-update-slice_fusion.r_0_, bf16[512,640]{1,0:T(8,128)(2,1)S(1)} %get-tuple-element.65.r_1_), custom_call_target="tpu_custom_call" | custom-call | flops 671088640 | bytes 6553600 | tf_op jit(solution)/shard_map/attend/pallas_call | solution.py:187
  66.1 5.6 %attend.5 = (f32[640,1024]{1,0:T(8,128)S(1)}, f32[16,1024]{1,0:T(8,128)S(1)}) custom-call(bf16[1024,640]{1,0:T(8,128)(2,1)S(1)} %constant_dynamic-update-slice_fusion.r_0_, bf16[512,640]{1,0:T(8,128)(2,1)S(1)} %collective-permute-done.3.r_1_, bf16[512,640]{1,0:T(8,128)(2,1)S(1)} %collective-permute-done.9.r_2_, ...), custom_call_target="tpu_custom_call", output_to_operand_aliasing={{0}: (3, {}), {1}: (4, {})} | custom-call | flops 1342177280 | bytes 6553600 | tf_op jit(solution)/shard_map/attend/pallas_call | solution.py:187
  71.7 5.6 %attend.6 = (f32[640,1024]{1,0:T(8,128)S(1)}, f32[16,1024]{1,0:T(8,128)S(1)}) custom-call(bf16[1024,640]{1,0:T(8,128)(2,1)S(1)} %constant_dynamic-update-slice_fusion.r_0_, bf16[512,640]{1,0:T(8,128)(2,1)S(1)} %collective-permute-done.10.r_1_, bf16[512,640]{1,0:T(8,128)(2,1)S(1)} %collective-permute-done.7.r_2_, ...), custom_call_target="tpu_custom_call", output_to_operand_aliasing={{0}: (3, {}), {1}: (4, {})} | custom-call | flops 1342177280 | bytes 6553600 | tf_op jit(solution)/shard_map/attend/pallas_call | solution.py:187
  77.4 0.1 fusion
  77.5 1.2 collective-permute-start.13
  78.7 0.3 collective-permute-start.12
  79.0 5.6 %attend.7 = (f32[640,1024]{1,0:T(8,128)S(1)}, f32[16,1024]{1,0:T(8,128)S(1)}) custom-call(bf16[1024,640]{1,0:T(8,128)(2,1)S(1)} %constant_dynamic-update-slice_fusion.r_0_, bf16[512,640]{1,0:T(8,128)(2,1)S(1)} %collective-permute-done.8.r_1_, bf16[512,640]{1,0:T(8,128)(2,1)S(1)} %collective-permute-done.11.r_2_, ...), custom_call_target="tpu_custom_call", output_to_operand_aliasing={{0}: (3, {}), {1}: (4, {})} | custom-call | flops 1342177280 | bytes 6553600 | tf_op jit(solution)/shard_map/attend/pallas_call | solution.py:187
  84.6 0.5 collective-permute-done.13.r_2_
  85.1 0.1 collective-permute-done.12.r_1_
  85.2 0.8 attend_last.3
  86.0 1.8 %attend_last.4 = (bf16[656,256]{1,0:T(8,128)(2,1)S(1)}, bf16[656,256]{1,0:T(8,128)(2,1)S(1)}) custom-call(bf16[1024,640]{1,0:T(8,128)(2,1)S(1)} %constant_dynamic-update-slice_fusion.r_0_, bf16[256,640]{1,0:T(8,128)(2,1)S(1)} %collective-permute-done.12.r_1_, bf16[256,640]{1,0:T(8,128)(2,1)S(1)} %collective-permute-done.13.r_2_, ...), custom_call_target="tpu_custom_call" | custom-call | flops 335544320 | bytes 2621440 | tf_op jit(solution)/shard_map/attend_last/pallas_call | solution.py:253
  87.7 0.1 collective-permute-start.14
  87.8 0.3 collective-permute-start.16
  88.1 3.0 %collective-permute-start.15 = (bf16[656,256]{1,0:T(8,128)(2,1)S(1)}, bf16[656,256]{1,0:T(8,128)(2,1)S(1)}, u32[]{:S(2)}, u32[]{:S(2)}) collective-permute-start(bf16[656,256]{1,0:T(8,128)(2,1)S(1)} %attend_last.3), channel_id=1, source_target_pairs={{0,16},{8,24},{16,0},{24,8},{1,17},{9,25},{17,1},{25,9},{2,18},{10... | collective-permute-start | bytes 1007624 | tf_op jit(solution)/shard_map/ppermute | solution.py:42
  91.1 0.8 attend_last.5.refs_0_
  91.9 2.0 %collective-permute-done.14.refs_1_ = bf16[656,256]{1,0:T(8,128)(2,1)S(1)} collective-permute-done((bf16[656,256]{1,0:T(8,128)(2,1)S(1)}, bf16[656,256]{1,0:T(8,128)(2,1)S(1)}, u32[]{:S(2)}, u32[]{:S(2)}) %collective-permute-start.14) | collective-permute-done | bytes 335904 | tf_op jit(solution)/shard_map/ppermute | solution.py:42
  93.8 5.2 %collective-permute-done.16.refs_3_ = bf16[656,256]{1,0:T(8,128)(2,1)S(1)} collective-permute-done((bf16[656,256]{1,0:T(8,128)(2,1)S(1)}, bf16[656,256]{1,0:T(8,128)(2,1)S(1)}, u32[]{:S(2)}, u32[]{:S(2)}) %collective-permute-start.16) | collective-permute-done | bytes 335904 | tf_op jit(solution)/shard_map/ppermute | solution.py:42
  99.1 0.9 collective-permute-done.15.refs_2_
  100.0 0.7 join.1.r_1_
  100.8 6.7 %collective-permute-start.17 = (bf16[256,640]{1,0:T(8,128)(2,1)S(1)}, bf16[256,640]{1,0:T(8,128)(2,1)S(1)}, u32[]{:S(2)}, u32[]{:S(2)}) collective-permute-start(bf16[256,640]{1,0:T(8,128)(2,1)S(1)} %join.1.r_1_), channel_id=1, source_target_pairs={{0,128},{128,0},{1,129},{129,1},{2,130},{130,2},{3,131},{131,3},{4... | collective-permute-start | bytes 983048 | tf_op jit(solution)/shard_map/ppermute | solution.py:50
  107.5 1.3 collective-permute-done.17.r_2_
  108.7 4.2 %project.1 = (bf16[128,1280]{1,0:T(8,128)(2,1)S(1)}, bf16[128,1280]{1,0:T(8,128)(2,1)S(1)}, bf16[128,1280]{1,0:T(8,128)(2,1)S(1)}, bf16[128,1280]{1,0:T(8,128)(2...) custom-call(s32[1]{0:T(128)} %bitcast.r_0_.c_ref, ...), custom_call_target="tpu_custom_call" | custom-call | tf_op jit(solution)/shard_map/project/pallas_call | solution.py:325
  112.9 0.0 copy-start.1
  112.9 0.0 copy-start.2
  112.9 0.2 collective-permute-start.23
  113.2 0.1 collective-permute-start.19
  113.3 1.5 %collective-permute-start.22 = (bf16[128,1280]{1,0:T(8,128)(2,1)S(1)}, bf16[128,1280]{1,0:T(8,128)(2,1)S(1)}, u32[]{:S(2)}, u32[]{:S(2)}) collective-permute-start(bf16[128,1280]{1,0:T(8,128)(2,1)S(1)} %get-tuple-element.52), channel_id=1, source_target_pairs={{0,32},{32,0},{64,96},{96,64},{1,33},{33,1},{65,97},{97,65},{2,34}... | collective-permute-start | bytes 983048 | tf_op jit(solution)/shard_map/ppermute | solution.py:38
  114.7 1.2 collective-permute-start.18
  115.9 2.6 %collective-permute-start.21 = (bf16[128,1280]{1,0:T(8,128)(2,1)S(1)}, bf16[128,1280]{1,0:T(8,128)(2,1)S(1)}, u32[]{:S(2)}, u32[]{:S(2)}) collective-permute-start(bf16[128,1280]{1,0:T(8,128)(2,1)S(1)} %get-tuple-element.58), channel_id=1, source_target_pairs={{0,96},{32,64},{64,32},{96,0},{1,97},{33,65},{65,33},{97,1},{2,98}... | collective-permute-start | bytes 983048 | tf_op jit(solution)/shard_map/ppermute | solution.py:38
  118.5 4.7 %collective-permute-done.23 = bf16[128,1280]{1,0:T(8,128)(2,1)S(1)} collective-permute-done((bf16[128,1280]{1,0:T(8,128)(2,1)S(1)}, bf16[128,1280]{1,0:T(8,128)(2,1)S(1)}, u32[]{:S(2)}, u32[]{:S(2)}) %collective-permute-start.23) | collective-permute-done | bytes 327712 | tf_op jit(solution)/shard_map/ppermute | solution.py:38
  123.2 0.1 add_convert_fusion
  123.2 0.1 collective-permute-start.24
  123.3 0.1 add_convert_fusion.1
  123.5 1.2 collective-permute-start.20
  124.6 5.6 %collective-permute-done.21.refs_3_ = bf16[128,1280]{1,0:T(8,128)(2,1)S(1)} collective-permute-done((bf16[128,1280]{1,0:T(8,128)(2,1)S(1)}, bf16[128,1280]{1,0:T(8,128)(2,1)S(1)}, u32[]{:S(2)}, u32[]{:S(2)}) %collective-permute-start.21) | collective-permute-done | bytes 327712 | tf_op jit(solution)/shard_map/ppermute | solution.py:38
  130.2 5.7 %collective-permute-done.24.refs_5_ = bf16[128,1280]{1,0:T(8,128)(2,1)S(1)} collective-permute-done((bf16[128,1280]{1,0:T(8,128)(2,1)S(1)}, bf16[128,1280]{1,0:T(8,128)(2,1)S(1)}, u32[]{:S(2)}, u32[]{:S(2)}) %collective-permute-start.24) | collective-permute-done | bytes 327712 | tf_op jit(solution)/shard_map/ppermute | solution.py:38
  135.9 1.3 collective-permute-done.20.refs_2_
  137.2 1.3 finish.1
  (22 shorter events, 0.4 us)
Async XLA Ops:
  3.7 6.9 %collective-permute-start = (bf16[192,640]{1,0:T(8,128)(2,1)}, bf16[192,640]{1,0:T(8,128)(2,1)S(1)}, u32[]{:S(2)}, u32[]{:S(2)}) collective-permute-start(bf16[192,640]{1,0:T(8,128)(2,1)} %get-tuple-element.34), channel_id=1, source_target_pairs={{0,32},{32,0},{64,96},{96,64},{1,33},{33,1},{65,97},{97,65},{2,34}... | collective-permute-start | bytes 737288 | tf_op jit(solution)/shard_map/ppermute | solution.py:38
  5.8 13.5 %collective-permute-start.1 = (bf16[192,640]{1,0:T(8,128)(2,1)}, bf16[192,640]{1,0:T(8,128)(2,1)S(1)}, u32[]{:S(2)}, u32[]{:S(2)}) collective-permute-start(bf16[192,640]{1,0:T(8,128)(2,1)} %get-tuple-element.35), channel_id=1, source_target_pairs={{0,64},{32,96},{64,0},{96,32},{1,65},{33,97},{65,1},{97,33},{2,66}... | collective-permute-start | bytes 737288 | tf_op jit(solution)/shard_map/ppermute | solution.py:38
  8.4 13.0 %collective-permute-start.2 = (bf16[192,640]{1,0:T(8,128)(2,1)}, bf16[192,640]{1,0:T(8,128)(2,1)S(1)}, u32[]{:S(2)}, u32[]{:S(2)}) collective-permute-start(bf16[192,640]{1,0:T(8,128)(2,1)} %get-tuple-element.36), channel_id=1, source_target_pairs={{0,96},{32,64},{64,32},{96,0},{1,97},{33,65},{65,33},{97,1},{2,98}... | collective-permute-start | bytes 737288 | tf_op jit(solution)/shard_map/ppermute | solution.py:38
  22.5 18.7 %collective-permute-start.9 = (bf16[512,640]{1,0:T(8,128)(2,1)S(1)}, bf16[512,640]{1,0:T(8,128)(2,1)S(1)}, u32[]{:S(2)}, u32[]{:S(2)}) collective-permute-start(bf16[512,640]{1,0:T(8,128)(2,1)S(1)} %get-tuple-element.65.r_1_), channel_id=1, source_target_pairs={{0,7},{1,2},{2,1},{3,4},{4,3},{5,6},{6,5},{7,0},{8,15},{9,10},{10,... | collective-permute-start | bytes 1966088 | tf_op jit(solution)/shard_map/ppermute | solution.py:46
  28.2 13.9 %collective-permute-start.3 = (bf16[512,640]{1,0:T(8,128)(2,1)S(1)}, bf16[512,640]{1,0:T(8,128)(2,1)S(1)}, u32[]{:S(2)}, u32[]{:S(2)}) collective-permute-start(bf16[512,640]{1,0:T(8,128)(2,1)S(1)} %get-tuple-element.65.r_1_), channel_id=1, source_target_pairs={{0,1},{1,0},{2,3},{3,2},{4,5},{5,4},{6,7},{7,6},{8,9},{9,8},{10,11... | collective-permute-start | bytes 1966088 | tf_op jit(solution)/shard_map/ppermute | solution.py:46
  41.2 15.6 %collective-permute-start.10 = (bf16[512,640]{1,0:T(8,128)(2,1)S(1)}, bf16[512,640]{1,0:T(8,128)(2,1)S(1)}, u32[]{:S(2)}, u32[]{:S(2)}) collective-permute-start(bf16[512,640]{1,0:T(8,128)(2,1)S(1)} %collective-permute-done.9.r_2_), channel_id=1, source_target_pairs={{0,1},{1,0},{2,3},{3,2},{4,5},{5,4},{6,7},{7,6},{8,9},{9,8},{10,11... | collective-permute-start | bytes 1966088 | tf_op jit(solution)/shard_map/ppermute | solution.py:46
  42.1 14.8 %collective-permute-start.7 = (bf16[512,640]{1,0:T(8,128)(2,1)S(1)}, bf16[512,640]{1,0:T(8,128)(2,1)S(1)}, u32[]{:S(2)}, u32[]{:S(2)}) collective-permute-start(bf16[512,640]{1,0:T(8,128)(2,1)S(1)} %collective-permute-done.3.r_1_), channel_id=1, source_target_pairs={{0,7},{1,2},{2,1},{3,4},{4,3},{5,6},{6,5},{7,0},{8,15},{9,10},{10,... | collective-permute-start | bytes 1966088 | tf_op jit(solution)/shard_map/ppermute | solution.py:46
  43.6 14.2 %collective-permute-start.4 = (bf16[256,640]{1,0:T(8,128)(2,1)S(1)}, bf16[256,640]{1,0:T(8,128)(2,1)S(1)}, u32[]{:S(2)}, u32[]{:S(2)}) collective-permute-start(bf16[256,640]{1,0:T(8,128)(2,1)S(1)} %pad_maximum_fusion), channel_id=1, source_target_pairs={{0,8},{8,0},{16,24},{24,16},{1,9},{9,1},{17,25},{25,17},{2,10},{10... | collective-permute-start | bytes 983048 | tf_op jit(solution)/shard_map/ppermute | solution.py:42
  44.9 13.7 %collective-permute-start.5 = (bf16[256,640]{1,0:T(8,128)(2,1)S(1)}, bf16[256,640]{1,0:T(8,128)(2,1)S(1)}, u32[]{:S(2)}, u32[]{:S(2)}) collective-permute-start(bf16[256,640]{1,0:T(8,128)(2,1)S(1)} %pad_maximum_fusion), channel_id=1, source_target_pairs={{0,16},{8,24},{16,0},{24,8},{1,17},{9,25},{17,1},{25,9},{2,18},{10... | collective-permute-start | bytes 983048 | tf_op jit(solution)/shard_map/ppermute | solution.py:42
  47.4 15.5 %collective-permute-start.6 = (bf16[256,640]{1,0:T(8,128)(2,1)S(1)}, bf16[256,640]{1,0:T(8,128)(2,1)S(1)}, u32[]{:S(2)}, u32[]{:S(2)}) collective-permute-start(bf16[256,640]{1,0:T(8,128)(2,1)S(1)} %pad_maximum_fusion), channel_id=1, source_target_pairs={{0,24},{8,16},{16,8},{24,0},{1,25},{9,17},{17,9},{25,1},{2,26},{10... | collective-permute-start | bytes 983048 | tf_op jit(solution)/shard_map/ppermute | solution.py:42
  56.8 20.6 %collective-permute-start.11 = (bf16[512,640]{1,0:T(8,128)(2,1)S(1)}, bf16[512,640]{1,0:T(8,128)(2,1)S(1)}, u32[]{:S(2)}, u32[]{:S(2)}) collective-permute-start(bf16[512,640]{1,0:T(8,128)(2,1)S(1)} %collective-permute-done.10.r_1_), channel_id=1, source_target_pairs={{0,7},{1,2},{2,1},{3,4},{4,3},{5,6},{6,5},{7,0},{8,15},{9,10},{10,... | collective-permute-start | bytes 1966088 | tf_op jit(solution)/shard_map/ppermute | solution.py:46
  56.9 20.5 %collective-permute-start.8 = (bf16[512,640]{1,0:T(8,128)(2,1)S(1)}, bf16[512,640]{1,0:T(8,128)(2,1)S(1)}, u32[]{:S(2)}, u32[]{:S(2)}) collective-permute-start(bf16[512,640]{1,0:T(8,128)(2,1)S(1)} %collective-permute-done.7.r_2_), channel_id=1, source_target_pairs={{0,1},{1,0},{2,3},{3,2},{4,5},{5,4},{6,7},{7,6},{8,9},{9,8},{10,11... | collective-permute-start | bytes 1966088 | tf_op jit(solution)/shard_map/ppermute | solution.py:46
  77.5 7.6 %collective-permute-start.13 = (bf16[256,640]{1,0:T(8,128)(2,1)S(1)}, bf16[256,640]{1,0:T(8,128)(2,1)S(1)}, u32[]{:S(2)}, u32[]{:S(2)}) collective-permute-start(bf16[256,640]{1,0:T(8,128)(2,1)S(1)} %pad_maximum_fusion.2), channel_id=1, source_target_pairs={{0,7},{1,2},{2,1},{3,4},{4,3},{5,6},{6,5},{7,0},{8,15},{9,10},{10,... | collective-permute-start | bytes 983048 | tf_op jit(solution)/shard_map/ppermute | solution.py:46
  78.7 6.5 %collective-permute-start.12 = (bf16[256,640]{1,0:T(8,128)(2,1)S(1)}, bf16[256,640]{1,0:T(8,128)(2,1)S(1)}, u32[]{:S(2)}, u32[]{:S(2)}) collective-permute-start(bf16[256,640]{1,0:T(8,128)(2,1)S(1)} %pad_maximum_fusion.1), channel_id=1, source_target_pairs={{0,1},{1,0},{2,3},{3,2},{4,5},{5,4},{6,7},{7,6},{8,9},{9,8},{10,11... | collective-permute-start | bytes 983048 | tf_op jit(solution)/shard_map/ppermute | solution.py:46
  87.7 6.1 %collective-permute-start.14 = (bf16[656,256]{1,0:T(8,128)(2,1)S(1)}, bf16[656,256]{1,0:T(8,128)(2,1)S(1)}, u32[]{:S(2)}, u32[]{:S(2)}) collective-permute-start(bf16[656,256]{1,0:T(8,128)(2,1)S(1)} %get-tuple-element.49), channel_id=1, source_target_pairs={{0,8},{8,0},{16,24},{24,16},{1,9},{9,1},{17,25},{25,17},{2,10},{10... | collective-permute-start | bytes 1007624 | tf_op jit(solution)/shard_map/ppermute | solution.py:42
  87.8 11.2 %collective-permute-start.16 = (bf16[656,256]{1,0:T(8,128)(2,1)S(1)}, bf16[656,256]{1,0:T(8,128)(2,1)S(1)}, u32[]{:S(2)}, u32[]{:S(2)}) collective-permute-start(bf16[656,256]{1,0:T(8,128)(2,1)S(1)} %get-tuple-element.51), channel_id=1, source_target_pairs={{0,24},{8,16},{16,8},{24,0},{1,25},{9,17},{17,9},{25,1},{2,26},{10... | collective-permute-start | bytes 1007624 | tf_op jit(solution)/shard_map/ppermute | solution.py:42
  88.1 11.9 %collective-permute-start.15 = (bf16[656,256]{1,0:T(8,128)(2,1)S(1)}, bf16[656,256]{1,0:T(8,128)(2,1)S(1)}, u32[]{:S(2)}, u32[]{:S(2)}) collective-permute-start(bf16[656,256]{1,0:T(8,128)(2,1)S(1)} %attend_last.3), channel_id=1, source_target_pairs={{0,16},{8,24},{16,0},{24,8},{1,17},{9,25},{17,1},{25,9},{2,18},{10... | collective-permute-start | bytes 1007624 | tf_op jit(solution)/shard_map/ppermute | solution.py:42
  100.8 8.0 %collective-permute-start.17 = (bf16[256,640]{1,0:T(8,128)(2,1)S(1)}, bf16[256,640]{1,0:T(8,128)(2,1)S(1)}, u32[]{:S(2)}, u32[]{:S(2)}) collective-permute-start(bf16[256,640]{1,0:T(8,128)(2,1)S(1)} %join.1.r_1_), channel_id=1, source_target_pairs={{0,128},{128,0},{1,129},{129,1},{2,130},{130,2},{3,131},{131,3},{4... | collective-permute-start | bytes 983048 | tf_op jit(solution)/shard_map/ppermute | solution.py:50
  108.7 4.4 %copy-start = (bf16[1,64,5120]{2,1,0:T(8,128)(2,1)S(1)}, bf16[1,64,5120]{2,1,0:T(8,128)(2,1)}, u32[]{:S(2)}) copy-start(bf16[1,64,5120]{2,1,0:T(8,128)(2,1)} %own_ref.1) | copy-start | bytes 1966084
  112.9 24.3 %copy-start.1 = (f32[5120]{0:T(1024)S(1)}, f32[5120]{0:T(1024)}, u32[]{:S(2)}) copy-start(f32[5120]{0:T(1024)} %gate_ref.1) | copy-start | bytes 61444
  112.9 24.3 %copy-start.2 = (f32[5120]{0:T(1024)S(1)}, f32[5120]{0:T(1024)}, u32[]{:S(2)}) copy-start(f32[5120]{0:T(1024)} %bias_ref.1) | copy-start | bytes 61444
  112.9 10.2 %collective-permute-start.23 = (bf16[128,1280]{1,0:T(8,128)(2,1)S(1)}, bf16[128,1280]{1,0:T(8,128)(2,1)S(1)}, u32[]{:S(2)}, u32[]{:S(2)}) collective-permute-start(bf16[128,1280]{1,0:T(8,128)(2,1)S(1)} %get-tuple-element.60), channel_id=1, source_target_pairs={{0,96},{32,64},{64,32},{96,0},{1,97},{33,65},{65,33},{97,1},{2,98}... | collective-permute-start | bytes 983048 | tf_op jit(solution)/shard_map/ppermute | solution.py:38
  113.2 10.2 %collective-permute-start.19 = (bf16[128,1280]{1,0:T(8,128)(2,1)S(1)}, bf16[128,1280]{1,0:T(8,128)(2,1)S(1)}, u32[]{:S(2)}, u32[]{:S(2)}) collective-permute-start(bf16[128,1280]{1,0:T(8,128)(2,1)S(1)} %get-tuple-element.57), channel_id=1, source_target_pairs={{0,32},{32,0},{64,96},{96,64},{1,33},{33,1},{65,97},{97,65},{2,34}... | collective-permute-start | bytes 983048 | tf_op jit(solution)/shard_map/ppermute | solution.py:38
  113.3 16.9 %collective-permute-start.22 = (bf16[128,1280]{1,0:T(8,128)(2,1)S(1)}, bf16[128,1280]{1,0:T(8,128)(2,1)S(1)}, u32[]{:S(2)}, u32[]{:S(2)}) collective-permute-start(bf16[128,1280]{1,0:T(8,128)(2,1)S(1)} %get-tuple-element.52), channel_id=1, source_target_pairs={{0,32},{32,0},{64,96},{96,64},{1,33},{33,1},{65,97},{97,65},{2,34}... | collective-permute-start | bytes 983048 | tf_op jit(solution)/shard_map/ppermute | solution.py:38
  114.7 9.9 %collective-permute-start.18 = (bf16[64,2560]{1,0:T(8,128)(2,1)S(1)}, bf16[64,2560]{1,0:T(8,128)(2,1)S(1)}, u32[]{:S(2)}, u32[]{:S(2)}) collective-permute-start(bf16[64,2560]{1,0:T(8,128)(2,1)S(1)} %dynamic-slice_bitcast_fusion), channel_id=1, source_target_pairs={{0,128},{128,0},{1,129},{129,1},{2,130},{130,2},{3,131},{131,3},{4... | collective-permute-start | bytes 983048 | tf_op jit(solution)/shard_map/ppermute | solution.py:50
  115.9 14.3 %collective-permute-start.21 = (bf16[128,1280]{1,0:T(8,128)(2,1)S(1)}, bf16[128,1280]{1,0:T(8,128)(2,1)S(1)}, u32[]{:S(2)}, u32[]{:S(2)}) collective-permute-start(bf16[128,1280]{1,0:T(8,128)(2,1)S(1)} %get-tuple-element.58), channel_id=1, source_target_pairs={{0,96},{32,64},{64,32},{96,0},{1,97},{33,65},{65,33},{97,1},{2,98}... | collective-permute-start | bytes 983048 | tf_op jit(solution)/shard_map/ppermute | solution.py:38
  123.2 12.7 %collective-permute-start.24 = (bf16[128,1280]{1,0:T(8,128)(2,1)S(1)}, bf16[128,1280]{1,0:T(8,128)(2,1)S(1)}, u32[]{:S(2)}, u32[]{:S(2)}) collective-permute-start(bf16[128,1280]{1,0:T(8,128)(2,1)S(1)} %add_convert_fusion), channel_id=1, source_target_pairs={{0,32},{32,0},{64,96},{96,64},{1,33},{33,1},{65,97},{97,65},{2,34}... | collective-permute-start | bytes 983048 | tf_op jit(solution)/shard_map/ppermute | solution.py:38
  123.5 13.7 %collective-permute-start.20 = (bf16[128,1280]{1,0:T(8,128)(2,1)S(1)}, bf16[128,1280]{1,0:T(8,128)(2,1)S(1)}, u32[]{:S(2)}, u32[]{:S(2)}) collective-permute-start(bf16[128,1280]{1,0:T(8,128)(2,1)S(1)} %add_convert_fusion.1), channel_id=1, source_target_pairs={{0,96},{32,64},{64,32},{96,0},{1,97},{33,65},{65,33},{97,1},{2,98}... | collective-permute-start | bytes 983048 | tf_op jit(solution)/shard_map/ppermute | solution.py:38
where the time goes:
time: 139 us; the launch traced here: 138 us
  waiting for transfers between devices  67.5 us (49%)
  starting transfers between devices  35.2 us (25%)
  Pallas kernels  32.5 us (23%)
  local copies, waits for them, and re-layouts  2.2 us (2%)
    ppermute x9, waiting for transfers between devices, swap_uly(): return lax.ppermute(a, 'uly', [(i, i ^ s) for i in range(ULY)])  29.4 us
    ppermute x8, waiting for transfers between devices, swap_z(): lax.ppermute(a, 'z', [(i, ((i - odd ^ 1) + odd) % ZS) for i in range(ZS)])  23.7 us
    pallas_call x4, Pallas kernels, attend(): pl.pallas_call(lambda *r: attend_body(len(kvs), state is None, *r), grid=...  20 us
    ppermute x6, waiting for transfers between devices, swap_x(): return lax.ppermute(a, 'x', [(i, i ^ s) for i in range(XS)])  13.1 us
    ppermute x9, starting transfers between devices, swap_uly(): return lax.ppermute(a, 'uly', [(i, i ^ s) for i in range(ULY)])  10.3 us
    ppermute x8, starting transfers between devices, swap_z(): lax.ppermute(a, 'z', [(i, ((i - odd ^ 1) + odd) % ZS) for i in range(ZS)])  9.65 us
    ppermute x2, starting transfers between devices, swap_cfg(): return lax.ppermute(a, 'cfg', [(0, 1), (1, 0)])  7.94 us
    ppermute x6, starting transfers between devices, swap_x(): return lax.ppermute(a, 'x', [(i, i ^ s) for i in range(XS)])  7.28 us
  transfers between devices with their start and end apart: 25, of which 18 were waited for; matrix products, arithmetic and copies ran while one was open for 1% of the time, Pallas kernels for 15%

commit v1 on v0

--- a/solution.py
+++ b/solution.py
@@ -27,7 +27,7 @@
 BF = jnp.bfloat16
 F32 = jnp.float32
 SCALE = math.log2(math.e) / math.sqrt(HEAD)
-VMEM = 48 * 1024 * 1024
+VMEM = 36 * 1024 * 1024
 
 
 def params(limit=VMEM):
@@ -74,56 +74,46 @@
     return jnp.cos(angle), jnp.where(even, -sine, 0.0), jnp.where(even, 0.0, sine)
 
 
-BLOCK = 3 * ROWS
-
-
-def prep_body(at_ref, proj_ref, q_gain, k_gain, rate_ref, *outs):
+def prep_body(width, at_ref, proj_ref, gain_ref, rate_ref, *outs):
     u = at_ref[0]
     cosine, s_even, s_odd = tables(at_ref[1], rate_ref[...])
-    gains = (q_gain, k_gain)
-
-    def scale_of(base):
-        total = jnp.zeros((ROWS, HEAD), F32)
-        for h in range(HEADS):
-            part = proj_ref[0, :, base + h * HEAD : base + (h + 1) * HEAD].astype(F32)
-            total = total + part * part
-        return lax.rsqrt(jnp.sum(total, axis=1, keepdims=True) * (1.0 / FEAT) + 1e-06)
-
-    scales = (scale_of(0), scale_of(FEAT))
-
-    def turned(which, at):
-        x = proj_ref[0, :, pl.ds(pl.multiple_of(which * FEAT + at, HEAD), HEAD)].astype(F32)
-        x = x * scales[which] * gains[which][pl.ds(at, HEAD)][None]
-        x = x * cosine + pltpu.roll(x, HEAD - 1, 1) * s_even + pltpu.roll(x, 1, 1) * s_odd
-        return x.astype(BF)
+    total = jnp.zeros((ROWS, HEAD), F32)
+    for h in range(HEADS):
+        part = proj_ref[0, :, h * HEAD : (h + 1) * HEAD].astype(F32)
+        total = total + part * part
+    scale = lax.rsqrt(jnp.sum(total, axis=1, keepdims=True) * (1.0 / FEAT) + 1e-06)
 
     for s in range(ULY):
         start = (u ^ s) * GF
         for h in range(GROUP):
-            here = slice(h * HEAD, (h + 1) * HEAD)
-            at = pl.multiple_of(start + h * HEAD, HEAD)
-            outs[s][0:ROWS, here] = turned(1, at)
-            outs[s][2 * ROWS :, here] = turned(0, at)
-        outs[s][ROWS : 2 * ROWS, :] = proj_ref[
-            0, :, pl.ds(pl.multiple_of(2 * FEAT + start, HEAD), GF)
-        ]
-
-
-def prep(place, projected, query_gain, key_gain):
+            at = pl.ds(pl.multiple_of(start + h * HEAD, HEAD), HEAD)
+            x = proj_ref[0, :, at].astype(F32)
+            x = x * scale * gain_ref[at][None]
+            x = x * cosine + pltpu.roll(x, HEAD - 1, 1) * s_even + pltpu.roll(x, 1, 1) * s_odd
+            outs[s][0:ROWS, h * HEAD : (h + 1) * HEAD] = x.astype(BF)
+        if width == 2:
+            outs[s][ROWS:, :] = proj_ref[0, :, pl.ds(pl.multiple_of(FEAT + start, HEAD), GF)]
+
+
+def prep(place, projected, gain, width):
     def whole(shape):
         return pl.BlockSpec(shape, lambda i: (0,) * len(shape))
 
+    part = pl.BlockSpec(
+        (pl.Element(1), pl.Element(ROWS), pl.Element(width * FEAT)),
+        lambda i: (0, 0, FEAT * (width - 1)),
+    )
     rate = jnp.asarray(rates())
-    args = (projected, query_gain, key_gain, rate)
-    return pl.pallas_call(
-        prep_body,
+    return pl.pallas_call(
+        lambda *r: prep_body(width, *r),
         grid=(1,),
-        in_specs=[pl.BlockSpec(memory_space=pltpu.SMEM)] + [whole(a.shape) for a in args],
-        out_specs=[whole((BLOCK, GF))] * ULY,
-        out_shape=[jax.ShapeDtypeStruct((BLOCK, GF), BF)] * ULY,
+        in_specs=[pl.BlockSpec(memory_space=pltpu.SMEM), part, whole(gain.shape), whole(rate.shape)],
+        out_specs=[whole((width * ROWS, GF))] * ULY,
+        out_shape=[jax.ShapeDtypeStruct((width * ROWS, GF), BF)] * ULY,
         compiler_params=params(62 * 1024 * 1024),
+        cost_estimate=pl.CostEstimate(flops=4000000, transcendentals=20000, bytes_accessed=2000000),
         name="prep",
-    )(place, *args)
+    )(place, projected, gain, rate)
 
 
 QB = 256
@@ -390,23 +380,26 @@
     c_arr = lax.axis_index("cfg").astype(jnp.int32)[None]
     first = ((u * XS + x) * ZS + lax.axis_index("z")) * ROWS
     place = jnp.stack([u, first]).astype(jnp.int32)
-    sent = prep(place, projected, query_gain, key_gain)
-
-    far = swap_uly(sent[2], 2)
-    got = [sent[0], swap_uly(sent[1], 1), far, swap_uly(sent[3], 3)]
-    own = jnp.concatenate([a[:ROWS] for a in got] + [a[ROWS : 2 * ROWS] for a in got], axis=0)
-    q_own = jnp.concatenate([a[2 * ROWS :] for a in got], axis=0)
+    def by_heads(sent):
+        far = swap_uly(sent[2], 2)
+        return [sent[0], swap_uly(sent[1], 1), far, swap_uly(sent[3], 3)]
+
+    got = by_heads(prep(place, projected, key_gain, 2))
+    own = jnp.concatenate([a[:ROWS] for a in got] + [a[ROWS:] for a in got], axis=0)
 
     left, right = swap_z(own, 0), swap_z(own, 1)
 
+    (place,) = after([place], own)
+    q_own = jnp.concatenate(by_heads(prep(place, projected, query_gain, 1)), axis=0)
     (q_sent,) = after([q_own], left)
-    q_far = swap_x(q_sent, 2)
-    q_all = jnp.concatenate([q_own, swap_x(q_sent, 1), q_far, swap_x(q_sent, 3)], axis=0)
+    q1, q3 = swap_x(q_sent, 1), swap_x(q_sent, 3)
+    q2 = [swap_x(q3[: QB // 2], 1), swap_x(q1[QB // 2 :], 3)]
+    q_all = jnp.concatenate([q_own, q1, *q2, q3], axis=0)
 
     left2, right2 = swap_z(right, 0), swap_z(left, 1)
-    left3, right3 = swap_z(right2, 0), swap_z(left2, 1)
     state = attend(q_all, [own])
     state = attend(q_all, [left, right], state)
+    left3, right3 = swap_z(right2, 0), swap_z(left2, 1)
     state = attend(q_all, [left2, right2], state)
     left3, right3 = after([left3, right3], *state)
     half = own.shape[0] // 2
@@ -414,6 +407,10 @@
     low = jnp.concatenate([left3[half // 2 : half], left3[half + half // 2 :]], axis=0)
     kvs = [swap_z(top, 0), swap_z(low, 1)]
     state = attend(q_all, [left3, right3], state)
+
+    residual_sent = lax.dynamic_slice(residual_in, (0, 0, (1 - c_arr[0]) * HALF), (1, ROWS, HALF))[0]
+    (residual_sent,) = after([residual_sent], left2)
+    residual_other = swap_cfg(residual_sent)
 
     (p2,) = attend_last(q_all, kvs, state, (2,))
     r2 = swap_x(p2, 2)
@@ -423,14 +420,13 @@
     (kv_b,) = after([kvs[0]], p1)
     (p0,) = attend_last(q_all, [kv_b, kvs[1]], state, (0,))
     mine = join([p0, r1, r2, r3])
+    (mine,) = after([mine], residual_other)
     heads = (mine, swap_cfg(mine))
 
-    p2a, p2b, p1a, p1b, p3a, p3b, p0a, p0b = project(c_arr, *heads, out_weight, (2, 1, 3, 0))
+    p2a, p2b = project(c_arr, *heads, out_weight, (2,))
     via_one = swap_uly(p2a, 1)
     via_three = swap_uly(p2b, 3)
-    residual_sent = lax.dynamic_slice(residual_in, (0, 0, (1 - c_arr[0]) * HALF), (1, ROWS, HALF))[0]
-    (residual_sent,) = after([residual_sent], p1a)
-    residual_other = swap_cfg(residual_sent)
+    p1a, p1b, p3a, p3b, p0a, p0b = project(c_arr, *heads, out_weight, (1, 3, 0))
     three_b = swap_uly(p3b, 3)
     one_a = swap_uly(p1a, 1)
     three_a = swap_uly(add(p3a, via_one), 3)

time: 139 us -> 135 us (0.971)
  waiting for transfers between devices: 67.5 us -> 39.3 us
  starting transfers between devices: 35.2 us -> 49.6 us
  local copies, waits for them, and re-layouts: 2.2 us -> 7.35 us
  other arithmetic: 0.92 us -> 3.26 us
  Pallas kernels: 32.5 us -> 34.7 us
    ppermute x8, waiting for transfers between devices: 23.7 us -> 4.92 us  [swap_z(): lax.ppermute(a, 'z', [(i, ((i - odd ^ 1) + odd) % ZS) for i in range(ZS)])]
    ppermute x6 -> x7, waiting for transfers between devices: 13.1 us -> 7.13 us  [swap_x(): return lax.ppermute(a, 'x', [(i, i ^ s) for i in range(XS)])]
    ppermute x2, starting transfers between devices: 7.94 us -> 13.8 us  [swap_cfg(): return lax.ppermute(a, 'cfg', [(0, 1), (1, 0)])]
    ppermute x8, starting transfers between devices: 9.65 us -> 15.3 us  [swap_z(): lax.ppermute(a, 'z', [(i, ((i - odd ^ 1) + odd) % ZS) for i in range(ZS)])]
    unnamed x15 -> x44, local copies, waits for them, and re-layouts: 2.05 us -> 7.19 us
    ppermute x9 -> x12, starting transfers between devices: 10.3 us -> 13.6 us  [swap_uly(): return lax.ppermute(a, 'uly', [(i, i ^ s) for i in range(ULY)])]
    ppermute x9 -> x12, waiting for transfers between devices: 29.4 us -> 26 us  [swap_uly(): return lax.ppermute(a, 'uly', [(i, i ^ s) for i in range(ULY)])]
    pallas_call x1 -> x2, Pallas kernels: 3 us -> 4.73 us  [prep(): pl.pallas_call(lambda *r: prep_body(width, *r), grid=(1,), in_specs=[pl.B...]
  transfers between devices with their start and end apart: 25 -> 29, of which waited for: 18 -> 13; matrix products, arithmetic and copies ran while one was open for 1% -> 3% of each run, Pallas kernels for 15% -> 22%
where the time goes in v1:
time: 135 us
  starting transfers between devices  49.6 us (37%)
  waiting for transfers between devices  39.3 us (29%)
  Pallas kernels  34.7 us (26%)
  local copies, waits for them, and re-layouts  7.35 us (5%)
  other arithmetic  3.26 us (2%)
    ppermute x12, waiting for transfers between devices, swap_uly(): return lax.ppermute(a, 'uly', [(i, i ^ s) for i in range(ULY)])  26 us
    pallas_call x4, Pallas kernels, attend(): pl.pallas_call(lambda *r: attend_body(len(kvs), state is None, *r), grid=...  21.1 us
    ppermute x8, starting transfers between devices, swap_z(): lax.ppermute(a, 'z', [(i, ((i - odd ^ 1) + odd) % ZS) for i in range(ZS)])  15.3 us
    ppermute x2, starting transfers between devices, swap_cfg(): return lax.ppermute(a, 'cfg', [(0, 1), (1, 0)])  13.8 us
    ppermute x12, starting transfers between devices, swap_uly(): return lax.ppermute(a, 'uly', [(i, i ^ s) for i in range(ULY)])  13.6 us
    unnamed x44, local copies, waits for them, and re-layouts  7.19 us
    ppermute x7, waiting for transfers between devices, swap_x(): return lax.ppermute(a, 'x', [(i, i ^ s) for i in range(XS)])  7.13 us
    ppermute x7, starting transfers between devices, swap_x(): return lax.ppermute(a, 'x', [(i, i ^ s) for i in range(XS)])  6.94 us
  transfers between devices with their start and end apart: 29, of which 13 were waited for; matrix products, arithmetic and copies ran while one was open for 3% of the time, Pallas kernels for 22%

profile of v1, /device:TPU:1, one launch (start us, length us, event | category | flops | bytes accessed | tf_op | source)
XLA Modules:
  0.0 134.7 jit_solution(10446692748289485199)
XLA Ops:
  0.0 0.7 pad_add_fusion.r_0_
  0.7 2.5 %prep.2 = (bf16[128,640]{1,0:T(8,128)(2,1)}, bf16[128,640]{1,0:T(8,128)(2,1)}, bf16[128,640]{1,0:T(8,128)(2,1)}, bf16[128,640]{1,0:T(8,128)(2,1)}) custom-call(s32[2]{0:T(128)} %pad_add_fusion.r_0_, bf16[1,64,7680]{2,1,0:T(8,128)(2,1)} %r_1_.3, f32[2560]{0:T(1024)} %r_2_.2, f32[1,128]{1,0:T(1,128)} %constant.33.clone.r_3_), custom_call_target="tpu_custom_call" | custom-call | flops 4000000 | bytes 2000000 | tf_op jit(solution)/shard_map/prep/pallas_call | solution.py:107
  3.1 2.1 %collective-permute-start = (bf16[128,640]{1,0:T(8,128)(2,1)}, bf16[128,640]{1,0:T(8,128)(2,1)S(1)}, u32[]{:S(2)}, u32[]{:S(2)}) collective-permute-start(bf16[128,640]{1,0:T(8,128)(2,1)} %get-tuple-element.40), channel_id=1, source_target_pairs={{0,32},{32,0},{64,96},{96,64},{1,33},{33,1},{65,97},{97,65},{2,34}... | collective-permute-start | bytes 491528 | tf_op jit(solution)/shard_map/ppermute | solution.py:38
  5.3 2.6 %collective-permute-start.1 = (bf16[128,640]{1,0:T(8,128)(2,1)}, bf16[128,640]{1,0:T(8,128)(2,1)S(1)}, u32[]{:S(2)}, u32[]{:S(2)}) collective-permute-start(bf16[128,640]{1,0:T(8,128)(2,1)} %get-tuple-element.41), channel_id=1, source_target_pairs={{0,64},{32,96},{64,0},{96,32},{1,65},{33,97},{65,1},{97,33},{2,66}... | collective-permute-start | bytes 491528 | tf_op jit(solution)/shard_map/ppermute | solution.py:38
  7.9 0.9 slice_dynamic-update-slice_fusion.7
  8.8 6.4 %collective-permute-done.1 = bf16[128,640]{1,0:T(8,128)(2,1)S(1)} collective-permute-done((bf16[128,640]{1,0:T(8,128)(2,1)}, bf16[128,640]{1,0:T(8,128)(2,1)S(1)}, u32[]{:S(2)}, u32[]{:S(2)}) %collective-permute-start.1) | collective-permute-done | bytes 163872 | tf_op jit(solution)/shard_map/ppermute | solution.py:38
  15.2 2.7 %collective-permute-done.2 = bf16[128,640]{1,0:T(8,128)(2,1)S(1)} collective-permute-done((bf16[128,640]{1,0:T(8,128)(2,1)}, bf16[128,640]{1,0:T(8,128)(2,1)S(1)}, u32[]{:S(2)}, u32[]{:S(2)}) %collective-permute-start.2) | collective-permute-done | bytes 163872 | tf_op jit(solution)/shard_map/ppermute | solution.py:38
  18.0 0.9 slice_dynamic-update-slice_fusion.6
  18.9 1.7 %collective-permute-start.9 = (bf16[512,640]{1,0:T(8,128)(2,1)S(1)}, bf16[512,640]{1,0:T(8,128)(2,1)S(1)}, u32[]{:S(2)}, u32[]{:S(2)}) collective-permute-start(bf16[512,640]{1,0:T(8,128)(2,1)S(1)} %slice_dynamic-update-slice_fusion.r_1_), channel_id=1, source_target_pairs={{0,1},{1,0},{2,3},{3,2},{4,5},{5,4},{6,7},{7,6},{8,9},{9,8},{10,11... | collective-permute-start | bytes 1966088 | tf_op jit(solution)/shard_map/ppermute | solution.py:46
  20.7 4.7 %collective-permute-start.3 = (bf16[512,640]{1,0:T(8,128)(2,1)S(1)}, bf16[512,640]{1,0:T(8,128)(2,1)}, u32[]{:S(2)}, u32[]{:S(2)}) collective-permute-start(bf16[512,640]{1,0:T(8,128)(2,1)S(1)} %slice_dynamic-update-slice_fusion.r_1_), channel_id=1, source_target_pairs={{0,7},{1,2},{2,1},{3,4},{4,3},{5,6},{6,5},{7,0},{8,15},{9,10},{10,... | collective-permute-start | bytes 1966088 | tf_op jit(solution)/shard_map/ppermute | solution.py:46
  25.3 2.3 %prep.3 = (bf16[64,640]{1,0:T(8,128)(2,1)}, bf16[64,640]{1,0:T(8,128)(2,1)}, bf16[64,640]{1,0:T(8,128)(2,1)}, bf16[64,640]{1,0:T(8,128)(2,1)}) custom-call(s32[2]{0:T(128)} %pad_add_fusion.r_0_, bf16[1,64,7680]{2,1,0:T(8,128)(2,1)} %r_1_.3, f32[2560]{0:T(1024)} %r_2_.3, f32[1,128]{1,0:T(1,128)} %constant.33.clone.r_3_), custom_call_target="tpu_custom_call" | custom-call | flops 4000000 | bytes 2000000 | tf_op jit(solution)/shard_map/prep/pallas_call | solution.py:107
  27.6 1.2 collective-permute-start.7
  28.8 2.7 %collective-permute-start.8 = (bf16[64,640]{1,0:T(8,128)(2,1)}, bf16[64,640]{1,0:T(8,128)(2,1)S(1)}, u32[]{:S(2)}, u32[]{:S(2)}) collective-permute-start(bf16[64,640]{1,0:T(8,128)(2,1)} %get-tuple-element.48), channel_id=1, source_target_pairs={{0,96},{32,64},{64,32},{96,0},{1,97},{33,65},{65,33},{97,1},{2,98}... | collective-permute-start | bytes 245768 | tf_op jit(solution)/shard_map/ppermute | solution.py:38
  31.4 2.9 %collective-permute-done.9.r_1_ = bf16[512,640]{1,0:T(8,128)(2,1)S(1)} collective-permute-done((bf16[512,640]{1,0:T(8,128)(2,1)S(1)}, bf16[512,640]{1,0:T(8,128)(2,1)S(1)}, u32[]{:S(2)}, u32[]{:S(2)}) %collective-permute-start.9) | collective-permute-done | bytes 655392 | tf_op jit(solution)/shard_map/ppermute | solution.py:46
  34.4 5.2 %collective-permute-start.14 = (bf16[512,640]{1,0:T(8,128)(2,1)S(1)}, bf16[512,640]{1,0:T(8,128)(2,1)S(1)}, u32[]{:S(2)}, u32[]{:S(2)}) collective-permute-start(bf16[512,640]{1,0:T(8,128)(2,1)S(1)} %collective-permute-done.9.r_1_), channel_id=1, source_target_pairs={{0,7},{1,2},{2,1},{3,4},{4,3},{5,6},{6,5},{7,0},{8,15},{9,10},{10,... | collective-permute-start | bytes 1966088 | tf_op jit(solution)/shard_map/ppermute | solution.py:46
  39.7 0.9 pad_maximum_fusion
  40.6 2.6 %collective-permute-start.11 = (bf16[256,640]{1,0:T(8,128)(2,1)S(1)}, bf16[256,640]{1,0:T(8,128)(2,1)S(1)}, u32[]{:S(2)}, u32[]{:S(2)}) collective-permute-start(bf16[256,640]{1,0:T(8,128)(2,1)S(1)} %pad_maximum_fusion), channel_id=1, source_target_pairs={{0,24},{8,16},{16,8},{24,0},{1,25},{9,17},{17,9},{25,1},{2,26},{10... | collective-permute-start | bytes 983048 | tf_op jit(solution)/shard_map/ppermute | solution.py:42
  43.1 0.9 constant_dynamic-update-slice_fusion.7
  44.1 4.6 %collective-permute-done.11 = bf16[256,640]{1,0:T(8,128)(2,1)S(1)} collective-permute-done((bf16[256,640]{1,0:T(8,128)(2,1)S(1)}, bf16[256,640]{1,0:T(8,128)(2,1)S(1)}, u32[]{:S(2)}, u32[]{:S(2)}) %collective-permute-start.11) | collective-permute-done | bytes 327712 | tf_op jit(solution)/shard_map/ppermute | solution.py:42
  48.7 0.1 collective-permute-start.12
  48.8 1.7 %collective-permute-done.10 = bf16[256,640]{1,0:T(8,128)(2,1)S(1)} collective-permute-done((bf16[256,640]{1,0:T(8,128)(2,1)S(1)}, bf16[256,640]{1,0:T(8,128)(2,1)S(1)}, u32[]{:S(2)}, u32[]{:S(2)}) %collective-permute-start.10) | collective-permute-done | bytes 327712 | tf_op jit(solution)/shard_map/ppermute | solution.py:42
  50.6 0.9 collective-permute-start.13
  51.5 1.1 collective-permute-done.14.r_2_
  52.5 0.2 collective-permute-start.15
  52.7 0.9 collective-permute-done.4.r_1_
  53.7 1.5 %collective-permute-start.16 = (bf16[512,640]{1,0:T(8,128)(2,1)S(1)}, bf16[512,640]{1,0:T(8,128)(2,1)S(1)}, u32[]{:S(2)}, u32[]{:S(2)}) collective-permute-start(bf16[512,640]{1,0:T(8,128)(2,1)S(1)} %collective-permute-done.4.r_1_), channel_id=1, source_target_pairs={{0,7},{1,2},{2,1},{3,4},{4,3},{5,6},{6,5},{7,0},{8,15},{9,10},{10,... | collective-permute-start | bytes 1966088 | tf_op jit(solution)/shard_map/ppermute | solution.py:46
  55.2 0.8 collective-permute-done.13
  56.1 3.2 %attend.4 = (f32[640,1024]{1,0:T(8,128)S(1)}, f32[16,1024]{1,0:T(8,128)S(1)}) custom-call(bf16[1024,640]{1,0:T(8,128)(2,1)S(1)} %constant_dynamic-update-slice_fusion.r_0_, bf16[512,640]{1,0:T(8,128)(2,1)S(1)} %copy-done.12), custom_call_target="tpu_custom_call" | custom-call | flops 671088640 | bytes 6553600 | tf_op jit(solution)/shard_map/attend/pallas_call | solution.py:177
  59.4 6.7 %attend.5 = (f32[640,1024]{1,0:T(8,128)S(1)}, f32[16,1024]{1,0:T(8,128)S(1)}) custom-call(bf16[1024,640]{1,0:T(8,128)(2,1)S(1)} %constant_dynamic-update-slice_fusion.r_0_, bf16[512,640]{1,0:T(8,128)(2,1)S(1)} %copy-done.8, bf16[512,640]{1,0:T(8,128)(2,1)} %collective-permute-done.3.r_2_, ...), custom_call_target="tpu_custom_call", output_to_operand_aliasing={{0}: (3, {}), {1}: (4, {})} | custom-call | flops 1342177280 | bytes 6553600 | tf_op jit(solution)/shard_map/attend/pallas_call | solution.py:177
  66.1 5.6 %attend.6 = (f32[640,1024]{1,0:T(8,128)S(1)}, f32[16,1024]{1,0:T(8,128)S(1)}) custom-call(bf16[1024,640]{1,0:T(8,128)(2,1)S(1)} %constant_dynamic-update-slice_fusion.r_0_, bf16[512,640]{1,0:T(8,128)(2,1)S(1)} %collective-permute-done.4.r_1_, bf16[512,640]{1,0:T(8,128)(2,1)S(1)} %collective-permute-done.14.r_2_, ...), custom_call_target="tpu_custom_call", output_to_operand_aliasing={{0}: (3, {}), {1}: (4, {})} | custom-call | flops 1342177280 | bytes 6553600 | tf_op jit(solution)/shard_map/attend/pallas_call | solution.py:177
  71.8 0.7 copy-done.2
  72.5 0.8 pad_maximum_fusion.2
  73.3 1.5 %collective-permute-start.18 = (bf16[256,640]{1,0:T(8,128)(2,1)}, bf16[256,640]{1,0:T(8,128)(2,1)S(1)}, u32[]{:S(2)}, u32[]{:S(2)}) collective-permute-start(bf16[256,640]{1,0:T(8,128)(2,1)} %pad_maximum_fusion.2), channel_id=1, source_target_pairs={{0,7},{1,2},{2,1},{3,4},{4,3},{5,6},{6,5},{7,0},{8,15},{9,10},{10,... | collective-permute-start | bytes 983048 | tf_op jit(solution)/shard_map/ppermute | solution.py:46
  74.8 0.8 pad_maximum_fusion.1
  75.6 0.3 collective-permute-start.17
  76.0 1.3 copy-done.1
  77.3 1.1 copy-done.3
  78.4 1.1 copy-done.5
  79.5 5.6 %attend.7 = (f32[640,1024]{1,0:T(8,128)S(1)}, f32[16,1024]{1,0:T(8,128)S(1)}) custom-call(bf16[1024,640]{1,0:T(8,128)(2,1)S(1)} %copy-done.1, bf16[512,640]{1,0:T(8,128)(2,1)S(1)} %copy-done.3, bf16[512,640]{1,0:T(8,128)(2,1)S(1)} %copy-done.5, f32[640,1024]{1,0:T(8,128)S(1)} %get-tuple-element.54.r_3_, ...), custom_call_target="tpu_custom_call", output_to_operand_aliasing={{0}: (3, {}), {1}: (4, {})} | custom-call | flops 1342177280 | bytes 6553600 | tf_op jit(solution)/shard_map/attend/pallas_call | solution.py:177
  85.1 0.8 attend_last.3
  85.9 1.3 collective-permute-start.20
  87.2 1.8 %attend_last.4 = (bf16[656,256]{1,0:T(8,128)(2,1)S(1)}, bf16[656,256]{1,0:T(8,128)(2,1)S(1)}) custom-call(bf16[1024,640]{1,0:T(8,128)(2,1)S(1)} %copy-done.1, bf16[256,640]{1,0:T(8,128)(2,1)S(1)} %collective-permute-done.17.r_1_, bf16[256,640]{1,0:T(8,128)(2,1)S(1)} %collective-permute-done.18.r_2_, f32[640,1024]{1,0:T(8,128)S(1)} %get-tuple-element.58.r_3_, ...), custom_call_target="tpu_custom_call" | custom-call | flops 335544320 | bytes 2621440 | tf_op jit(solution)/shard_map/attend_last/pallas_call | solution.py:243
  88.9 0.4 collective-permute-start.19
  89.3 1.7 %collective-permute-start.21 = (bf16[656,256]{1,0:T(8,128)(2,1)S(1)}, bf16[656,256]{1,0:T(8,128)(2,1)S(1)}, u32[]{:S(2)}, u32[]{:S(2)}) collective-permute-start(bf16[656,256]{1,0:T(8,128)(2,1)S(1)} %get-tuple-element.63), channel_id=1, source_target_pairs={{0,24},{8,16},{16,8},{24,0},{1,25},{9,17},{17,9},{25,1},{2,26},{10... | collective-permute-start | bytes 1007624 | tf_op jit(solution)/shard_map/ppermute | solution.py:42
  91.1 8.3 %collective-permute-start.5 = (bf16[64,2560]{1,0:T(8,128)(2,1)S(1)}, bf16[64,2560]{1,0:T(8,128)(2,1)S(1)}, u32[]{:S(2)}, u32[]{:S(2)}) collective-permute-start(bf16[64,2560]{1,0:T(8,128)(2,1)S(1)} %dynamic-slice_bitcast_fusion), channel_id=1, source_target_pairs={{0,128},{128,0},{1,129},{129,1},{2,130},{130,2},{3,131},{131,3},{4... | collective-permute-start | bytes 983048 | tf_op jit(solution)/shard_map/ppermute | solution.py:50
  99.4 0.8 attend_last.5.refs_0_
  100.2 0.8 join.1.r_1_
  101.0 5.5 %collective-permute-start.22 = (bf16[256,640]{1,0:T(8,128)(2,1)S(1)}, bf16[256,640]{1,0:T(8,128)(2,1)S(1)}, u32[]{:S(2)}, u32[]{:S(2)}) collective-permute-start(bf16[256,640]{1,0:T(8,128)(2,1)S(1)} %join.1.r_1_), channel_id=1, source_target_pairs={{0,128},{128,0},{1,129},{129,1},{2,130},{130,2},{3,131},{131,3},{4... | collective-permute-start | bytes 983048 | tf_op jit(solution)/shard_map/ppermute | solution.py:50
  106.5 1.3 collective-permute-done.22.r_2_
  107.7 1.2 project.3
  108.9 0.3 collective-permute-start.27
  109.2 0.1 collective-permute-start.23
  109.3 2.3 %project.2 = (bf16[128,1280]{1,0:T(8,128)(2,1)S(1)}, bf16[128,1280]{1,0:T(8,128)(2,1)S(1)}, bf16[128,1280]{1,0:T(8,128)(2,1)S(1)}, bf16[128,1280]{1,0:T(8,128)(2...) custom-call(s32[1]{0:T(128)} %bitcast.r_0_.c_ref, bf16[256,640]{1,0:T(8,128)(2,1)S(1)} %join.1.r_1_, ...), custom_call_target="tpu_custom_call" | custom-call | tf_op jit(solution)/shard_map/project/pallas_call | solution.py:315
  111.7 2.6 %collective-permute-start.25 = (bf16[128,1280]{1,0:T(8,128)(2,1)S(1)}, bf16[128,1280]{1,0:T(8,128)(2,1)S(1)}, u32[]{:S(2)}, u32[]{:S(2)}) collective-permute-start(bf16[128,1280]{1,0:T(8,128)(2,1)S(1)} %get-tuple-element.69), channel_id=1, source_target_pairs={{0,96},{32,64},{64,32},{96,0},{1,97},{33,65},{65,33},{97,1},{2,98}... | collective-permute-start | bytes 983048 | tf_op jit(solution)/shard_map/ppermute | solution.py:38
  114.3 0.9 collective-permute-start.26
  115.2 4.1 %collective-permute-done.27 = bf16[128,1280]{1,0:T(8,128)(2,1)S(1)} collective-permute-done((bf16[128,1280]{1,0:T(8,128)(2,1)S(1)}, bf16[128,1280]{1,0:T(8,128)(2,1)S(1)}, u32[]{:S(2)}, u32[]{:S(2)}) %collective-permute-start.27) | collective-permute-done | bytes 327712 | tf_op jit(solution)/shard_map/ppermute | solution.py:38
  119.3 0.1 add_convert_fusion
  119.4 0.1 collective-permute-start.28
  119.5 0.1 add_convert_fusion.1
  119.6 1.0 collective-permute-start.24
  120.7 5.7 %collective-permute-done.25.refs_3_ = bf16[128,1280]{1,0:T(8,128)(2,1)S(1)} collective-permute-done((bf16[128,1280]{1,0:T(8,128)(2,1)S(1)}, bf16[128,1280]{1,0:T(8,128)(2,1)S(1)}, u32[]{:S(2)}, u32[]{:S(2)}) %collective-permute-start.25) | collective-permute-done | bytes 327712 | tf_op jit(solution)/shard_map/ppermute | solution.py:38
  126.4 5.7 %collective-permute-done.28.refs_5_ = bf16[128,1280]{1,0:T(8,128)(2,1)S(1)} collective-permute-done((bf16[128,1280]{1,0:T(8,128)(2,1)S(1)}, bf16[128,1280]{1,0:T(8,128)(2,1)S(1)}, u32[]{:S(2)}, u32[]{:S(2)}) %collective-permute-start.28) | collective-permute-done | bytes 327712 | tf_op jit(solution)/shard_map/ppermute | solution.py:38
  132.0 1.4 %collective-permute-done.24.refs_2_ = bf16[128,1280]{1,0:T(8,128)(2,1)S(1)} collective-permute-done((bf16[128,1280]{1,0:T(8,128)(2,1)S(1)}, bf16[128,1280]{1,0:T(8,128)(2,1)S(1)}, u32[]{:S(2)}, u32[]{:S(2)}) %collective-permute-start.24) | collective-permute-done | bytes 327712 | tf_op jit(solution)/shard_map/ppermute | solution.py:38
  133.4 1.3 finish.1
  (64 shorter events, 0.5 us)
Async XLA Ops:
  3.1 5.6 %collective-permute-start = (bf16[128,640]{1,0:T(8,128)(2,1)}, bf16[128,640]{1,0:T(8,128)(2,1)S(1)}, u32[]{:S(2)}, u32[]{:S(2)}) collective-permute-start(bf16[128,640]{1,0:T(8,128)(2,1)} %get-tuple-element.40), channel_id=1, source_target_pairs={{0,32},{32,0},{64,96},{96,64},{1,33},{33,1},{65,97},{97,65},{2,34}... | collective-permute-start | bytes 491528 | tf_op jit(solution)/shard_map/ppermute | solution.py:38
  5.3 10.0 %collective-permute-start.1 = (bf16[128,640]{1,0:T(8,128)(2,1)}, bf16[128,640]{1,0:T(8,128)(2,1)S(1)}, u32[]{:S(2)}, u32[]{:S(2)}) collective-permute-start(bf16[128,640]{1,0:T(8,128)(2,1)} %get-tuple-element.41), channel_id=1, source_target_pairs={{0,64},{32,96},{64,0},{96,32},{1,65},{33,97},{65,1},{97,33},{2,66}... | collective-permute-start | bytes 491528 | tf_op jit(solution)/shard_map/ppermute | solution.py:38
  7.9 10.1 %collective-permute-start.2 = (bf16[128,640]{1,0:T(8,128)(2,1)}, bf16[128,640]{1,0:T(8,128)(2,1)S(1)}, u32[]{:S(2)}, u32[]{:S(2)}) collective-permute-start(bf16[128,640]{1,0:T(8,128)(2,1)} %get-tuple-element.42), channel_id=1, source_target_pairs={{0,96},{32,64},{64,32},{96,0},{1,97},{33,65},{65,33},{97,1},{2,98}... | collective-permute-start | bytes 491528 | tf_op jit(solution)/shard_map/ppermute | solution.py:38
  18.9 29.9 %copy-start.11 = (bf16[512,640]{1,0:T(8,128)(2,1)}, bf16[512,640]{1,0:T(8,128)(2,1)S(1)}, u32[]{:S(2)}) copy-start(bf16[512,640]{1,0:T(8,128)(2,1)S(1)} %slice_dynamic-update-slice_fusion.r_1_) | copy-start | bytes 1966084
  18.9 15.5 %collective-permute-start.9 = (bf16[512,640]{1,0:T(8,128)(2,1)S(1)}, bf16[512,640]{1,0:T(8,128)(2,1)S(1)}, u32[]{:S(2)}, u32[]{:S(2)}) collective-permute-start(bf16[512,640]{1,0:T(8,128)(2,1)S(1)} %slice_dynamic-update-slice_fusion.r_1_), channel_id=1, source_target_pairs={{0,1},{1,0},{2,3},{3,2},{4,5},{5,4},{6,7},{7,6},{8,9},{9,8},{10,11... | collective-permute-start | bytes 1966088 | tf_op jit(solution)/shard_map/ppermute | solution.py:46
  20.7 19.0 %collective-permute-start.3 = (bf16[512,640]{1,0:T(8,128)(2,1)S(1)}, bf16[512,640]{1,0:T(8,128)(2,1)}, u32[]{:S(2)}, u32[]{:S(2)}) collective-permute-start(bf16[512,640]{1,0:T(8,128)(2,1)S(1)} %slice_dynamic-update-slice_fusion.r_1_), channel_id=1, source_target_pairs={{0,7},{1,2},{2,1},{3,4},{4,3},{5,6},{6,5},{7,0},{8,15},{9,10},{10,... | collective-permute-start | bytes 1966088 | tf_op jit(solution)/shard_map/ppermute | solution.py:46
  27.6 12.0 %collective-permute-start.6 = (bf16[64,640]{1,0:T(8,128)(2,1)}, bf16[64,640]{1,0:T(8,128)(2,1)S(1)}, u32[]{:S(2)}, u32[]{:S(2)}) collective-permute-start(bf16[64,640]{1,0:T(8,128)(2,1)} %get-tuple-element.46), channel_id=1, source_target_pairs={{0,32},{32,0},{64,96},{96,64},{1,33},{33,1},{65,97},{97,65},{2,34}... | collective-permute-start | bytes 245768 | tf_op jit(solution)/shard_map/ppermute | solution.py:38
  27.6 12.0 %collective-permute-start.7 = (bf16[64,640]{1,0:T(8,128)(2,1)}, bf16[64,640]{1,0:T(8,128)(2,1)S(1)}, u32[]{:S(2)}, u32[]{:S(2)}) collective-permute-start(bf16[64,640]{1,0:T(8,128)(2,1)} %get-tuple-element.47), channel_id=1, source_target_pairs={{0,64},{32,96},{64,0},{96,32},{1,65},{33,97},{65,1},{97,33},{2,66}... | collective-permute-start | bytes 245768 | tf_op jit(solution)/shard_map/ppermute | solution.py:38
  28.8 10.9 %collective-permute-start.8 = (bf16[64,640]{1,0:T(8,128)(2,1)}, bf16[64,640]{1,0:T(8,128)(2,1)S(1)}, u32[]{:S(2)}, u32[]{:S(2)}) collective-permute-start(bf16[64,640]{1,0:T(8,128)(2,1)} %get-tuple-element.48), channel_id=1, source_target_pairs={{0,96},{32,64},{64,32},{96,0},{1,97},{33,65},{65,33},{97,1},{2,98}... | collective-permute-start | bytes 245768 | tf_op jit(solution)/shard_map/ppermute | solution.py:38
  34.4 17.1 %copy-start.7 = (bf16[512,640]{1,0:T(8,128)(2,1)}, bf16[512,640]{1,0:T(8,128)(2,1)S(1)}, u32[]{:S(2)}) copy-start(bf16[512,640]{1,0:T(8,128)(2,1)S(1)} %collective-permute-done.9.r_1_) | copy-start | bytes 1966084
  34.4 18.1 %collective-permute-start.14 = (bf16[512,640]{1,0:T(8,128)(2,1)S(1)}, bf16[512,640]{1,0:T(8,128)(2,1)S(1)}, u32[]{:S(2)}, u32[]{:S(2)}) collective-permute-start(bf16[512,640]{1,0:T(8,128)(2,1)S(1)} %collective-permute-done.9.r_1_), channel_id=1, source_target_pairs={{0,7},{1,2},{2,1},{3,4},{4,3},{5,6},{6,5},{7,0},{8,15},{9,10},{10,... | collective-permute-start | bytes 1966088 | tf_op jit(solution)/shard_map/ppermute | solution.py:46
  39.6 14.0 %collective-permute-start.4 = (bf16[512,640]{1,0:T(8,128)(2,1)}, bf16[512,640]{1,0:T(8,128)(2,1)S(1)}, u32[]{:S(2)}, u32[]{:S(2)}) collective-permute-start(bf16[512,640]{1,0:T(8,128)(2,1)} %collective-permute-done.3.r_2_), channel_id=1, source_target_pairs={{0,1},{1,0},{2,3},{3,2},{4,5},{5,4},{6,7},{7,6},{8,9},{9,8},{10,11... | collective-permute-start | bytes 1966088 | tf_op jit(solution)/shard_map/ppermute | solution.py:46
  40.6 8.1 %collective-permute-start.11 = (bf16[256,640]{1,0:T(8,128)(2,1)S(1)}, bf16[256,640]{1,0:T(8,128)(2,1)S(1)}, u32[]{:S(2)}, u32[]{:S(2)}) collective-permute-start(bf16[256,640]{1,0:T(8,128)(2,1)S(1)} %pad_maximum_fusion), channel_id=1, source_target_pairs={{0,24},{8,16},{16,8},{24,0},{1,25},{9,17},{17,9},{25,1},{2,26},{10... | collective-permute-start | bytes 983048 | tf_op jit(solution)/shard_map/ppermute | solution.py:42
  44.0 6.5 %collective-permute-start.10 = (bf16[256,640]{1,0:T(8,128)(2,1)S(1)}, bf16[256,640]{1,0:T(8,128)(2,1)S(1)}, u32[]{:S(2)}, u32[]{:S(2)}) collective-permute-start(bf16[256,640]{1,0:T(8,128)(2,1)S(1)} %pad_maximum_fusion), channel_id=1, source_target_pairs={{0,8},{8,0},{16,24},{24,16},{1,9},{9,1},{17,25},{25,17},{2,10},{10... | collective-permute-start | bytes 983048 | tf_op jit(solution)/shard_map/ppermute | solution.py:42
  48.7 6.5 %collective-permute-start.12 = (bf16[128,640]{1,0:T(8,128)(2,1)S(1)}, bf16[128,640]{1,0:T(8,128)(2,1)S(1)}, u32[]{:S(2)}, u32[]{:S(2)}) collective-permute-start(bf16[128,640]{1,0:T(8,128)(2,1)S(1)} %slice.62), channel_id=1, source_target_pairs={{0,8},{8,0},{16,24},{24,16},{1,9},{9,1},{17,25},{25,17},{2,10},{10... | collective-permute-start | bytes 491528 | tf_op jit(solution)/shard_map/ppermute | solution.py:42
  50.6 5.6 %copy-start.12 = (bf16[512,640]{1,0:T(8,128)(2,1)S(1)}, bf16[512,640]{1,0:T(8,128)(2,1)}, u32[]{:S(2)}) copy-start(bf16[512,640]{1,0:T(8,128)(2,1)} %copy-done.11) | copy-start | bytes 1966084
  50.6 5.5 %collective-permute-start.13 = (bf16[128,640]{1,0:T(8,128)(2,1)S(1)}, bf16[128,640]{1,0:T(8,128)(2,1)S(1)}, u32[]{:S(2)}, u32[]{:S(2)}) collective-permute-start(bf16[128,640]{1,0:T(8,128)(2,1)S(1)} %slice.63), channel_id=1, source_target_pairs={{0,24},{8,16},{16,8},{24,0},{1,25},{9,17},{17,9},{25,1},{2,26},{10... | collective-permute-start | bytes 491528 | tf_op jit(solution)/shard_map/ppermute | solution.py:42
  52.5 19.2 %collective-permute-start.15 = (bf16[512,640]{1,0:T(8,128)(2,1)S(1)}, bf16[512,640]{1,0:T(8,128)(2,1)S(1)}, u32[]{:S(2)}, u32[]{:S(2)}) collective-permute-start(bf16[512,640]{1,0:T(8,128)(2,1)S(1)} %collective-permute-done.14.r_2_), channel_id=1, source_target_pairs={{0,1},{1,0},{2,3},{3,2},{4,5},{5,4},{6,7},{7,6},{8,9},{9,8},{10,11... | collective-permute-start | bytes 1966088 | tf_op jit(solution)/shard_map/ppermute | solution.py:46
  53.7 18.1 %collective-permute-start.16 = (bf16[512,640]{1,0:T(8,128)(2,1)S(1)}, bf16[512,640]{1,0:T(8,128)(2,1)S(1)}, u32[]{:S(2)}, u32[]{:S(2)}) collective-permute-start(bf16[512,640]{1,0:T(8,128)(2,1)S(1)} %collective-permute-done.4.r_1_), channel_id=1, source_target_pairs={{0,7},{1,2},{2,1},{3,4},{4,3},{5,6},{6,5},{7,0},{8,15},{9,10},{10,... | collective-permute-start | bytes 1966088 | tf_op jit(solution)/shard_map/ppermute | solution.py:46
  56.1 9.9 %copy-start = (bf16[1024,640]{1,0:T(8,128)(2,1)}, bf16[1024,640]{1,0:T(8,128)(2,1)S(1)}, u32[]{:S(2)}) copy-start(bf16[1024,640]{1,0:T(8,128)(2,1)S(1)} %constant_dynamic-update-slice_fusion.r_0_) | copy-start | bytes 3932164
  56.1 3.2 %copy-start.8 = (bf16[512,640]{1,0:T(8,128)(2,1)S(1)}, bf16[512,640]{1,0:T(8,128)(2,1)}, u32[]{:S(2)}) copy-start(bf16[512,640]{1,0:T(8,128)(2,1)} %copy-done.7) | copy-start | bytes 1966084
  71.7 0.8 copy-start.2
  71.7 3.9 %copy-start.4 = (bf16[512,640]{1,0:T(8,128)(2,1)}, bf16[512,640]{1,0:T(8,128)(2,1)S(1)}, u32[]{:S(2)}) copy-start(bf16[512,640]{1,0:T(8,128)(2,1)S(1)} %collective-permute-done.16.r_2_) | copy-start | bytes 1966084
  73.3 11.8 %collective-permute-start.18 = (bf16[256,640]{1,0:T(8,128)(2,1)}, bf16[256,640]{1,0:T(8,128)(2,1)S(1)}, u32[]{:S(2)}, u32[]{:S(2)}) collective-permute-start(bf16[256,640]{1,0:T(8,128)(2,1)} %pad_maximum_fusion.2), channel_id=1, source_target_pairs={{0,7},{1,2},{2,1},{3,4},{4,3},{5,6},{6,5},{7,0},{8,15},{9,10},{10,... | collective-permute-start | bytes 983048 | tf_op jit(solution)/shard_map/ppermute | solution.py:46
  75.6 9.4 %collective-permute-start.17 = (bf16[256,640]{1,0:T(8,128)(2,1)}, bf16[256,640]{1,0:T(8,128)(2,1)S(1)}, u32[]{:S(2)}, u32[]{:S(2)}) collective-permute-start(bf16[256,640]{1,0:T(8,128)(2,1)} %pad_maximum_fusion.1), channel_id=1, source_target_pairs={{0,1},{1,0},{2,3},{3,2},{4,5},{5,4},{6,7},{7,6},{8,9},{9,8},{10,11... | collective-permute-start | bytes 983048 | tf_op jit(solution)/shard_map/ppermute | solution.py:46
  76.0 1.3 copy-start.1
  77.3 1.1 copy-start.3
  78.4 1.1 copy-start.5
  85.1 22.6 %slice-start = ((s8[6553600]{0:T(1024)(128)(4,1)}), s8[4194304]{0:T(1024)(128)(4,1)S(1)}, s32[]{:S(2)}) async-start(s8[6553600]{0:T(1024)(128)(4,1)} %bitcast.5), calls=%async_computation | async-start | bytes 8388608
  85.9 5.2 %copy-start.6 = (bf16[1,64,5120]{2,1,0:T(8,128)(2,1)S(1)}, bf16[1,64,5120]{2,1,0:T(8,128)(2,1)}, u32[]{:S(2)}) copy-start(bf16[1,64,5120]{2,1,0:T(8,128)(2,1)} %own_ref.1) | copy-start | bytes 1966084
  85.9 21.8 %slice-start.1 = ((s8[6553600]{0:T(1024)(128)(4,1)}), s8[2359296]{0:T(1024)(128)(4,1)S(1)}, s32[]{:S(2)}) async-start(s8[6553600]{0:T(1024)(128)(4,1)} %bitcast.5), calls=%async_computation.1 | async-start | bytes 4718592
  85.9 14.3 %collective-permute-start.20 = (bf16[656,256]{1,0:T(8,128)(2,1)S(1)}, bf16[656,256]{1,0:T(8,128)(2,1)S(1)}, u32[]{:S(2)}, u32[]{:S(2)}) collective-permute-start(bf16[656,256]{1,0:T(8,128)(2,1)S(1)} %attend_last.3), channel_id=1, source_target_pairs={{0,16},{8,24},{16,0},{24,8},{1,17},{9,25},{17,1},{25,9},{2,18},{10... | collective-permute-start | bytes 1007624 | tf_op jit(solution)/shard_map/ppermute | solution.py:42
  88.9 11.2 %collective-permute-start.19 = (bf16[656,256]{1,0:T(8,128)(2,1)S(1)}, bf16[656,256]{1,0:T(8,128)(2,1)S(1)}, u32[]{:S(2)}, u32[]{:S(2)}) collective-permute-start(bf16[656,256]{1,0:T(8,128)(2,1)S(1)} %get-tuple-element.61), channel_id=1, source_target_pairs={{0,8},{8,0},{16,24},{24,16},{1,9},{9,1},{17,25},{25,17},{2,10},{10... | collective-permute-start | bytes 1007624 | tf_op jit(solution)/shard_map/ppermute | solution.py:42
  89.3 10.8 %collective-permute-start.21 = (bf16[656,256]{1,0:T(8,128)(2,1)S(1)}, bf16[656,256]{1,0:T(8,128)(2,1)S(1)}, u32[]{:S(2)}, u32[]{:S(2)}) collective-permute-start(bf16[656,256]{1,0:T(8,128)(2,1)S(1)} %get-tuple-element.63), channel_id=1, source_target_pairs={{0,24},{8,16},{16,8},{24,0},{1,25},{9,17},{17,9},{25,1},{2,26},{10... | collective-permute-start | bytes 1007624 | tf_op jit(solution)/shard_map/ppermute | solution.py:42
  91.1 9.9 %collective-permute-start.5 = (bf16[64,2560]{1,0:T(8,128)(2,1)S(1)}, bf16[64,2560]{1,0:T(8,128)(2,1)S(1)}, u32[]{:S(2)}, u32[]{:S(2)}) collective-permute-start(bf16[64,2560]{1,0:T(8,128)(2,1)S(1)} %dynamic-slice_bitcast_fusion), channel_id=1, source_target_pairs={{0,128},{128,0},{1,129},{129,1},{2,130},{130,2},{3,131},{131,3},{4... | collective-permute-start | bytes 983048 | tf_op jit(solution)/shard_map/ppermute | solution.py:50
  101.0 6.7 %collective-permute-start.22 = (bf16[256,640]{1,0:T(8,128)(2,1)S(1)}, bf16[256,640]{1,0:T(8,128)(2,1)S(1)}, u32[]{:S(2)}, u32[]{:S(2)}) collective-permute-start(bf16[256,640]{1,0:T(8,128)(2,1)S(1)} %join.1.r_1_), channel_id=1, source_target_pairs={{0,128},{128,0},{1,129},{129,1},{2,130},{130,2},{3,131},{131,3},{4... | collective-permute-start | bytes 983048 | tf_op jit(solution)/shard_map/ppermute | solution.py:50
  108.9 10.4 %collective-permute-start.27 = (bf16[128,1280]{1,0:T(8,128)(2,1)S(1)}, bf16[128,1280]{1,0:T(8,128)(2,1)S(1)}, u32[]{:S(2)}, u32[]{:S(2)}) collective-permute-start(bf16[128,1280]{1,0:T(8,128)(2,1)S(1)} %get-tuple-element.72), channel_id=1, source_target_pairs={{0,96},{32,64},{64,32},{96,0},{1,97},{33,65},{65,33},{97,1},{2,98}... | collective-permute-start | bytes 983048 | tf_op jit(solution)/shard_map/ppermute | solution.py:38
  109.2 10.3 %collective-permute-start.23 = (bf16[128,1280]{1,0:T(8,128)(2,1)S(1)}, bf16[128,1280]{1,0:T(8,128)(2,1)S(1)}, u32[]{:S(2)}, u32[]{:S(2)}) collective-permute-start(bf16[128,1280]{1,0:T(8,128)(2,1)S(1)} %get-tuple-element.68), channel_id=1, source_target_pairs={{0,32},{32,0},{64,96},{96,64},{1,33},{33,1},{65,97},{97,65},{2,34}... | collective-permute-start | bytes 983048 | tf_op jit(solution)/shard_map/ppermute | solution.py:38
  111.7 21.7 %copy-start.9 = (f32[5120]{0:T(1024)S(1)}, f32[5120]{0:T(1024)}, u32[]{:S(2)}) copy-start(f32[5120]{0:T(1024)} %gate_ref.1) | copy-start | bytes 61444
  111.7 21.7 %copy-start.10 = (f32[5120]{0:T(1024)S(1)}, f32[5120]{0:T(1024)}, u32[]{:S(2)}) copy-start(f32[5120]{0:T(1024)} %bias_ref.1) | copy-start | bytes 61444
  111.7 14.7 %collective-permute-start.25 = (bf16[128,1280]{1,0:T(8,128)(2,1)S(1)}, bf16[128,1280]{1,0:T(8,128)(2,1)S(1)}, u32[]{:S(2)}, u32[]{:S(2)}) collective-permute-start(bf16[128,1280]{1,0:T(8,128)(2,1)S(1)} %get-tuple-element.69), channel_id=1, source_target_pairs={{0,96},{32,64},{64,32},{96,0},{1,97},{33,65},{65,33},{97,1},{2,98}... | collective-permute-start | bytes 983048 | tf_op jit(solution)/shard_map/ppermute | solution.py:38
  114.3 12.0 %collective-permute-start.26 = (bf16[128,1280]{1,0:T(8,128)(2,1)S(1)}, bf16[128,1280]{1,0:T(8,128)(2,1)S(1)}, u32[]{:S(2)}, u32[]{:S(2)}) collective-permute-start(bf16[128,1280]{1,0:T(8,128)(2,1)S(1)} %get-tuple-element.70), channel_id=1, source_target_pairs={{0,32},{32,0},{64,96},{96,64},{1,33},{33,1},{65,97},{97,65},{2,34}... | collective-permute-start | bytes 983048 | tf_op jit(solution)/shard_map/ppermute | solution.py:38
  119.4 12.6 %collective-permute-start.28 = (bf16[128,1280]{1,0:T(8,128)(2,1)S(1)}, bf16[128,1280]{1,0:T(8,128)(2,1)S(1)}, u32[]{:S(2)}, u32[]{:S(2)}) collective-permute-start(bf16[128,1280]{1,0:T(8,128)(2,1)S(1)} %add_convert_fusion), channel_id=1, source_target_pairs={{0,32},{32,0},{64,96},{96,64},{1,33},{33,1},{65,97},{97,65},{2,34}... | collective-permute-start | bytes 983048 | tf_op jit(solution)/shard_map/ppermute | solution.py:38
  119.6 13.8 %collective-permute-start.24 = (bf16[128,1280]{1,0:T(8,128)(2,1)S(1)}, bf16[128,1280]{1,0:T(8,128)(2,1)S(1)}, u32[]{:S(2)}, u32[]{:S(2)}) collective-permute-start(bf16[128,1280]{1,0:T(8,128)(2,1)S(1)} %add_convert_fusion.1), channel_id=1, source_target_pairs={{0,96},{32,64},{64,32},{96,0},{1,97},{33,65},{65,33},{97,1},{2,98}... | collective-permute-start | bytes 983048 | tf_op jit(solution)/shard_map/ppermute | solution.py:38

commit v2 on v1

--- a/solution.py
+++ b/solution.py
@@ -119,10 +119,13 @@
 QB = 256
 
 
-def heads_step(q, kvs, h, m_old):
+def heads_step(q, kvs, h, m_old, apart=False):
     here = slice(h * HEAD, (h + 1) * HEAD)
-    keys = jnp.concatenate([kv[0 : kv.shape[0] // 2, here] for kv in kvs], axis=0)
-    vals = jnp.concatenate([kv[kv.shape[0] // 2 :, here] for kv in kvs], axis=0)
+    if apart:
+        keys, vals = (kv[:, here] for kv in kvs)
+    else:
+        keys = jnp.concatenate([kv[0 : kv.shape[0] // 2, here] for kv in kvs], axis=0)
+        vals = jnp.concatenate([kv[kv.shape[0] // 2 :, here] for kv in kvs], axis=0)
     s = lax.dot_general(keys, q[:, here], (((1,), (1,)), ((), ())), preferred_element_type=F32)
     m = jnp.max(s, axis=0, keepdims=True) * SCALE
     if m_old is not None:
@@ -203,7 +206,7 @@
     parts = []
     for h in range(GROUP):
         m_old = ml_in[h : h + 1, :]
-        m, l, o = heads_step(q_ref, kv_refs, h, m_old)
+        m, l, o = heads_step(q_ref, kv_refs, h, m_old, True)
         here = slice(h * HEAD, (h + 1) * HEAD)
         alpha = jnp.exp2(m_old - m)
         l = l + alpha * ml_in[8 + h : 9 + h, :]
@@ -401,10 +404,8 @@
     state = attend(q_all, [left, right], state)
     left3, right3 = swap_z(right2, 0), swap_z(left2, 1)
     state = attend(q_all, [left2, right2], state)
-    left3, right3 = after([left3, right3], *state)
     half = own.shape[0] // 2
-    top = jnp.concatenate([right3[: half // 2], right3[half : half + half // 2]], axis=0)
-    low = jnp.concatenate([left3[half // 2 : half], left3[half + half // 2 :]], axis=0)
+    top, low = after([right3[:half], left3[half:]], *state)
     kvs = [swap_z(top, 0), swap_z(low, 1)]
     state = attend(q_all, [left3, right3], state)
 

time: 135 us -> 134 us (level)
  other arithmetic: 3.26 us -> 1.72 us
    slice x1 -> x2, local copies, waits for them, and re-layouts: 0.06 us -> 1.63 us  [on_device(): top, low = after([right3[:half], left3[half:]], *state)]
    concatenate x2 -> x0, other arithmetic: 1.53 us -> none  [the longest x1 0.78 us: on_device(): jnp.concatenate([right3[:half // 2], right3[half:half + half // 2]], axis=0)]
    unnamed x44 -> x48, local copies, waits for them, and re-layouts: 7.19 us -> 6.59 us
  transfers between devices with their start and end apart: 29 -> 29, of which waited for: 13 -> 12; matrix products, arithmetic and copies ran while one was open for 3% -> 3% of each run, Pallas kernels for 22% -> 21%
where the time goes in v2:
time: 134 us
  starting transfers between devices  50.2 us (37%)
  waiting for transfers between devices  39.2 us (29%)
  Pallas kernels  33.6 us (25%)
  local copies, waits for them, and re-layouts  8.33 us (6%)
  other arithmetic  1.72 us (1%)
    ppermute x12, waiting for transfers between devices, swap_uly(): return lax.ppermute(a, 'uly', [(i, i ^ s) for i in range(ULY)])  26 us
    pallas_call x4, Pallas kernels, attend(): pl.pallas_call(lambda *r: attend_body(len(kvs), state is None, *r), grid=...  20 us
    ppermute x8, starting transfers between devices, swap_z(): lax.ppermute(a, 'z', [(i, ((i - odd ^ 1) + odd) % ZS) for i in range(ZS)])  16.1 us
    ppermute x2, starting transfers between devices, swap_cfg(): return lax.ppermute(a, 'cfg', [(0, 1), (1, 0)])  13.8 us
    ppermute x12, starting transfers between devices, swap_uly(): return lax.ppermute(a, 'uly', [(i, i ^ s) for i in range(ULY)])  13.4 us
    ppermute x7, waiting for transfers between devices, swap_x(): return lax.ppermute(a, 'x', [(i, i ^ s) for i in range(XS)])  7.24 us
    ppermute x7, starting transfers between devices, swap_x(): return lax.ppermute(a, 'x', [(i, i ^ s) for i in range(XS)])  6.94 us
    unnamed x48, local copies, waits for them, and re-layouts  6.59 us
  transfers between devices with their start and end apart: 29, of which 12 were waited for; matrix products, arithmetic and copies ran while one was open for 3% of the time, Pallas kernels for 21%

profile of v2, /device:TPU:1, one launch (start us, length us, event | category | flops | bytes accessed | tf_op | source)
XLA Modules:
  0.0 133.6 jit_solution(8094417371437650048)
XLA Ops:
  0.0 0.6 pad_add_fusion.r_0_
  0.6 2.5 %prep.2 = (bf16[128,640]{1,0:T(8,128)(2,1)}, bf16[128,640]{1,0:T(8,128)(2,1)}, bf16[128,640]{1,0:T(8,128)(2,1)}, bf16[128,640]{1,0:T(8,128)(2,1)}) custom-call(s32[2]{0:T(128)} %pad_add_fusion.r_0_, bf16[1,64,7680]{2,1,0:T(8,128)(2,1)} %r_1_.3, f32[2560]{0:T(1024)} %r_2_.2, f32[1,128]{1,0:T(1,128)} %constant.33.clone.r_3_), custom_call_target="tpu_custom_call" | custom-call | flops 4000000 | bytes 2000000 | tf_op jit(solution)/shard_map/prep/pallas_call | solution.py:107
  3.0 2.1 %collective-permute-start = (bf16[128,640]{1,0:T(8,128)(2,1)}, bf16[128,640]{1,0:T(8,128)(2,1)S(1)}, u32[]{:S(2)}, u32[]{:S(2)}) collective-permute-start(bf16[128,640]{1,0:T(8,128)(2,1)} %get-tuple-element.40), channel_id=1, source_target_pairs={{0,32},{32,0},{64,96},{96,64},{1,33},{33,1},{65,97},{97,65},{2,34}... | collective-permute-start | bytes 491528 | tf_op jit(solution)/shard_map/ppermute | solution.py:38
  5.2 2.6 %collective-permute-start.1 = (bf16[128,640]{1,0:T(8,128)(2,1)}, bf16[128,640]{1,0:T(8,128)(2,1)S(1)}, u32[]{:S(2)}, u32[]{:S(2)}) collective-permute-start(bf16[128,640]{1,0:T(8,128)(2,1)} %get-tuple-element.41), channel_id=1, source_target_pairs={{0,64},{32,96},{64,0},{96,32},{1,65},{33,97},{65,1},{97,33},{2,66}... | collective-permute-start | bytes 491528 | tf_op jit(solution)/shard_map/ppermute | solution.py:38
  7.8 0.9 slice_dynamic-update-slice_fusion.7
  8.7 6.4 %collective-permute-done.1 = bf16[128,640]{1,0:T(8,128)(2,1)S(1)} collective-permute-done((bf16[128,640]{1,0:T(8,128)(2,1)}, bf16[128,640]{1,0:T(8,128)(2,1)S(1)}, u32[]{:S(2)}, u32[]{:S(2)}) %collective-permute-start.1) | collective-permute-done | bytes 163872 | tf_op jit(solution)/shard_map/ppermute | solution.py:38
  15.2 2.7 %collective-permute-done.2 = bf16[128,640]{1,0:T(8,128)(2,1)S(1)} collective-permute-done((bf16[128,640]{1,0:T(8,128)(2,1)}, bf16[128,640]{1,0:T(8,128)(2,1)S(1)}, u32[]{:S(2)}, u32[]{:S(2)}) %collective-permute-start.2) | collective-permute-done | bytes 163872 | tf_op jit(solution)/shard_map/ppermute | solution.py:38
  17.9 0.9 slice_dynamic-update-slice_fusion.6
  18.8 1.7 %collective-permute-start.9 = (bf16[512,640]{1,0:T(8,128)(2,1)S(1)}, bf16[512,640]{1,0:T(8,128)(2,1)S(1)}, u32[]{:S(2)}, u32[]{:S(2)}) collective-permute-start(bf16[512,640]{1,0:T(8,128)(2,1)S(1)} %slice_dynamic-update-slice_fusion.r_1_), channel_id=1, source_target_pairs={{0,1},{1,0},{2,3},{3,2},{4,5},{5,4},{6,7},{7,6},{8,9},{9,8},{10,11... | collective-permute-start | bytes 1966088 | tf_op jit(solution)/shard_map/ppermute | solution.py:46
  20.6 4.7 %collective-permute-start.3 = (bf16[512,640]{1,0:T(8,128)(2,1)S(1)}, bf16[512,640]{1,0:T(8,128)(2,1)S(1)}, u32[]{:S(2)}, u32[]{:S(2)}) collective-permute-start(bf16[512,640]{1,0:T(8,128)(2,1)S(1)} %slice_dynamic-update-slice_fusion.r_1_), channel_id=1, source_target_pairs={{0,7},{1,2},{2,1},{3,4},{4,3},{5,6},{6,5},{7,0},{8,15},{9,10},{10,... | collective-permute-start | bytes 1966088 | tf_op jit(solution)/shard_map/ppermute | solution.py:46
  25.2 2.3 %prep.3 = (bf16[64,640]{1,0:T(8,128)(2,1)}, bf16[64,640]{1,0:T(8,128)(2,1)}, bf16[64,640]{1,0:T(8,128)(2,1)}, bf16[64,640]{1,0:T(8,128)(2,1)}) custom-call(s32[2]{0:T(128)} %pad_add_fusion.r_0_, bf16[1,64,7680]{2,1,0:T(8,128)(2,1)} %r_1_.3, f32[2560]{0:T(1024)} %r_2_.3, f32[1,128]{1,0:T(1,128)} %constant.33.clone.r_3_), custom_call_target="tpu_custom_call" | custom-call | flops 4000000 | bytes 2000000 | tf_op jit(solution)/shard_map/prep/pallas_call | solution.py:107
  27.5 1.2 collective-permute-start.7
  28.7 2.7 %collective-permute-start.8 = (bf16[64,640]{1,0:T(8,128)(2,1)}, bf16[64,640]{1,0:T(8,128)(2,1)S(1)}, u32[]{:S(2)}, u32[]{:S(2)}) collective-permute-start(bf16[64,640]{1,0:T(8,128)(2,1)} %get-tuple-element.48), channel_id=1, source_target_pairs={{0,96},{32,64},{64,32},{96,0},{1,97},{33,65},{65,33},{97,1},{2,98}... | collective-permute-start | bytes 245768 | tf_op jit(solution)/shard_map/ppermute | solution.py:38
  31.4 2.9 %collective-permute-done.9.r_1_ = bf16[512,640]{1,0:T(8,128)(2,1)S(1)} collective-permute-done((bf16[512,640]{1,0:T(8,128)(2,1)S(1)}, bf16[512,640]{1,0:T(8,128)(2,1)S(1)}, u32[]{:S(2)}, u32[]{:S(2)}) %collective-permute-start.9) | collective-permute-done | bytes 655392 | tf_op jit(solution)/shard_map/ppermute | solution.py:46
  34.2 5.2 %collective-permute-start.15 = (bf16[512,640]{1,0:T(8,128)(2,1)S(1)}, bf16[512,640]{1,0:T(8,128)(2,1)S(1)}, u32[]{:S(2)}, u32[]{:S(2)}) collective-permute-start(bf16[512,640]{1,0:T(8,128)(2,1)S(1)} %collective-permute-done.9.r_1_), channel_id=1, source_target_pairs={{0,7},{1,2},{2,1},{3,4},{4,3},{5,6},{6,5},{7,0},{8,15},{9,10},{10,... | collective-permute-start | bytes 1966088 | tf_op jit(solution)/shard_map/ppermute | solution.py:46
  39.5 1.0 pad_maximum_fusion
  40.5 2.6 %collective-permute-start.11 = (bf16[256,640]{1,0:T(8,128)(2,1)S(1)}, bf16[256,640]{1,0:T(8,128)(2,1)S(1)}, u32[]{:S(2)}, u32[]{:S(2)}) collective-permute-start(bf16[256,640]{1,0:T(8,128)(2,1)S(1)} %pad_maximum_fusion), channel_id=1, source_target_pairs={{0,24},{8,16},{16,8},{24,0},{1,25},{9,17},{17,9},{25,1},{2,26},{10... | collective-permute-start | bytes 983048 | tf_op jit(solution)/shard_map/ppermute | solution.py:42
  43.1 0.9 constant_dynamic-update-slice_fusion.7
  44.0 4.5 %collective-permute-done.11 = bf16[256,640]{1,0:T(8,128)(2,1)S(1)} collective-permute-done((bf16[256,640]{1,0:T(8,128)(2,1)S(1)}, bf16[256,640]{1,0:T(8,128)(2,1)S(1)}, u32[]{:S(2)}, u32[]{:S(2)}) %collective-permute-start.11) | collective-permute-done | bytes 327712 | tf_op jit(solution)/shard_map/ppermute | solution.py:42
  48.5 0.1 collective-permute-start.12
  48.6 1.7 %collective-permute-done.10 = bf16[256,640]{1,0:T(8,128)(2,1)S(1)} collective-permute-done((bf16[256,640]{1,0:T(8,128)(2,1)S(1)}, bf16[256,640]{1,0:T(8,128)(2,1)S(1)}, u32[]{:S(2)}, u32[]{:S(2)}) %collective-permute-start.10) | collective-permute-done | bytes 327712 | tf_op jit(solution)/shard_map/ppermute | solution.py:42
  50.4 0.9 collective-permute-start.13
  51.3 1.8 %collective-permute-done.4.r_1_ = bf16[512,640]{1,0:T(8,128)(2,1)S(1)} collective-permute-done((bf16[512,640]{1,0:T(8,128)(2,1)S(1)}, bf16[512,640]{1,0:T(8,128)(2,1)S(1)}, u32[]{:S(2)}, u32[]{:S(2)}) %collective-permute-start.4) | collective-permute-done | bytes 655392 | tf_op jit(solution)/shard_map/ppermute | solution.py:46
  53.1 1.7 %collective-permute-start.14 = (bf16[512,640]{1,0:T(8,128)(2,1)S(1)}, bf16[512,640]{1,0:T(8,128)(2,1)S(1)}, u32[]{:S(2)}, u32[]{:S(2)}) collective-permute-start(bf16[512,640]{1,0:T(8,128)(2,1)S(1)} %collective-permute-done.4.r_1_), channel_id=1, source_target_pairs={{0,7},{1,2},{2,1},{3,4},{4,3},{5,6},{6,5},{7,0},{8,15},{9,10},{10,... | collective-permute-start | bytes 1966088 | tf_op jit(solution)/shard_map/ppermute | solution.py:46
  54.8 0.0 collective-permute-done.12
  54.9 1.0 collective-permute-done.13
  56.0 3.2 %attend.4 = (f32[640,1024]{1,0:T(8,128)S(1)}, f32[16,1024]{1,0:T(8,128)S(1)}) custom-call(bf16[1024,640]{1,0:T(8,128)(2,1)S(1)} %constant_dynamic-update-slice_fusion.r_0_, bf16[512,640]{1,0:T(8,128)(2,1)S(1)} %copy-done.14), custom_call_target="tpu_custom_call" | custom-call | flops 671088640 | bytes 6553600 | tf_op jit(solution)/shard_map/attend/pallas_call | solution.py:180
  59.2 5.6 %attend.5 = (f32[640,1024]{1,0:T(8,128)S(1)}, f32[16,1024]{1,0:T(8,128)S(1)}) custom-call(bf16[1024,640]{1,0:T(8,128)(2,1)S(1)} %constant_dynamic-update-slice_fusion.r_0_, bf16[512,640]{1,0:T(8,128)(2,1)S(1)} %copy-done.8, bf16[512,640]{1,0:T(8,128)(2,1)S(1)} %copy-done.10, ...), custom_call_target="tpu_custom_call", output_to_operand_aliasing={{0}: (3, {}), {1}: (4, {})} | custom-call | flops 1342177280 | bytes 6553600 | tf_op jit(solution)/shard_map/attend/pallas_call | solution.py:180
  64.8 5.6 %attend.6 = (f32[640,1024]{1,0:T(8,128)S(1)}, f32[16,1024]{1,0:T(8,128)S(1)}) custom-call(bf16[1024,640]{1,0:T(8,128)(2,1)S(1)} %constant_dynamic-update-slice_fusion.r_0_, bf16[512,640]{1,0:T(8,128)(2,1)S(1)} %collective-permute-done.4.r_1_, bf16[512,640]{1,0:T(8,128)(2,1)S(1)} %collective-permute-done.15.r_2_, ...), custom_call_target="tpu_custom_call", output_to_operand_aliasing={{0}: (3, {}), {1}: (4, {})} | custom-call | flops 1342177280 | bytes 6553600 | tf_op jit(solution)/shard_map/attend/pallas_call | solution.py:180
  70.5 0.8 slice.56
  71.3 0.8 slice.57
  72.1 0.1 copy-done.4
  72.2 1.2 collective-permute-start.17
  73.4 1.6 %collective-permute-start.18 = (bf16[256,640]{1,0:T(8,128)(2,1)}, bf16[256,640]{1,0:T(8,128)(2,1)S(1)}, u32[]{:S(2)}, u32[]{:S(2)}) collective-permute-start(bf16[256,640]{1,0:T(8,128)(2,1)} %slice.57), channel_id=1, source_target_pairs={{0,7},{1,2},{2,1},{3,4},{4,3},{5,6},{6,5},{7,0},{8,15},{9,10},{10,... | collective-permute-start | bytes 983048 | tf_op jit(solution)/shard_map/ppermute | solution.py:46
  75.0 1.3 copy-done.1
  76.4 1.1 copy-done.3
  77.5 1.1 copy-done.5
  78.5 5.6 %attend.7 = (f32[640,1024]{1,0:T(8,128)S(1)}, f32[16,1024]{1,0:T(8,128)S(1)}) custom-call(bf16[1024,640]{1,0:T(8,128)(2,1)S(1)} %copy-done.1, bf16[512,640]{1,0:T(8,128)(2,1)S(1)} %copy-done.5, bf16[512,640]{1,0:T(8,128)(2,1)S(1)} %copy-done.3, f32[640,1024]{1,0:T(8,128)S(1)} %get-tuple-element.54.r_3_, ...), custom_call_target="tpu_custom_call", output_to_operand_aliasing={{0}: (3, {}), {1}: (4, {})} | custom-call | flops 1342177280 | bytes 6553600 | tf_op jit(solution)/shard_map/attend/pallas_call | solution.py:180
  84.2 0.8 attend_last.3
  85.0 0.0 slice-start.1
  85.0 1.5 %collective-permute-start.20 = (bf16[656,256]{1,0:T(8,128)(2,1)S(1)}, bf16[656,256]{1,0:T(8,128)(2,1)S(1)}, u32[]{:S(2)}, u32[]{:S(2)}) collective-permute-start(bf16[656,256]{1,0:T(8,128)(2,1)S(1)} %attend_last.3), channel_id=1, source_target_pairs={{0,16},{8,24},{16,0},{24,8},{1,17},{9,25},{17,1},{25,9},{2,18},{10... | collective-permute-start | bytes 1007624 | tf_op jit(solution)/shard_map/ppermute | solution.py:42
  86.5 1.8 %attend_last.4 = (bf16[656,256]{1,0:T(8,128)(2,1)S(1)}, bf16[656,256]{1,0:T(8,128)(2,1)S(1)}) custom-call(bf16[1024,640]{1,0:T(8,128)(2,1)S(1)} %copy-done.1, bf16[256,640]{1,0:T(8,128)(2,1)S(1)} %collective-permute-done.17.r_1_, bf16[256,640]{1,0:T(8,128)(2,1)S(1)} %collective-permute-done.18.r_2_, f32[640,1024]{1,0:T(8,128)S(1)} %get-tuple-element.58.r_3_, ...), custom_call_target="tpu_custom_call" | custom-call | flops 335544320 | bytes 2621440 | tf_op jit(solution)/shard_map/attend_last/pallas_call | solution.py:246
  88.3 0.4 collective-permute-start.19
  88.6 1.5 %collective-permute-start.21 = (bf16[656,256]{1,0:T(8,128)(2,1)S(1)}, bf16[656,256]{1,0:T(8,128)(2,1)S(1)}, u32[]{:S(2)}, u32[]{:S(2)}) collective-permute-start(bf16[656,256]{1,0:T(8,128)(2,1)S(1)} %get-tuple-element.63), channel_id=1, source_target_pairs={{0,24},{8,16},{16,8},{24,0},{1,25},{9,17},{17,9},{25,1},{2,26},{10... | collective-permute-start | bytes 1007624 | tf_op jit(solution)/shard_map/ppermute | solution.py:42
  90.2 8.3 %collective-permute-start.5 = (bf16[64,2560]{1,0:T(8,128)(2,1)S(1)}, bf16[64,2560]{1,0:T(8,128)(2,1)S(1)}, u32[]{:S(2)}, u32[]{:S(2)}) collective-permute-start(bf16[64,2560]{1,0:T(8,128)(2,1)S(1)} %dynamic-slice_bitcast_fusion), channel_id=1, source_target_pairs={{0,128},{128,0},{1,129},{129,1},{2,130},{130,2},{3,131},{131,3},{4... | collective-permute-start | bytes 983048 | tf_op jit(solution)/shard_map/ppermute | solution.py:50
  98.5 0.8 attend_last.5.refs_0_
  99.3 0.8 join.1.r_1_
  100.1 5.5 %collective-permute-start.22 = (bf16[256,640]{1,0:T(8,128)(2,1)S(1)}, bf16[256,640]{1,0:T(8,128)(2,1)S(1)}, u32[]{:S(2)}, u32[]{:S(2)}) collective-permute-start(bf16[256,640]{1,0:T(8,128)(2,1)S(1)} %join.1.r_1_), channel_id=1, source_target_pairs={{0,128},{128,0},{1,129},{129,1},{2,130},{130,2},{3,131},{131,3},{4... | collective-permute-start | bytes 983048 | tf_op jit(solution)/shard_map/ppermute | solution.py:50
  105.6 1.3 collective-permute-done.22.r_2_
  106.8 1.2 project.3
  108.0 0.1 collective-permute-start.27
  108.1 0.3 collective-permute-start.23
  108.4 2.3 %project.2 = (bf16[128,1280]{1,0:T(8,128)(2,1)S(1)}, bf16[128,1280]{1,0:T(8,128)(2,1)S(1)}, bf16[128,1280]{1,0:T(8,128)(2,1)S(1)}, bf16[128,1280]{1,0:T(8,128)(2...) custom-call(s32[1]{0:T(128)} %bitcast.r_0_.c_ref, bf16[256,640]{1,0:T(8,128)(2,1)S(1)} %join.1.r_1_, ...), custom_call_target="tpu_custom_call" | custom-call | tf_op jit(solution)/shard_map/project/pallas_call | solution.py:318
  110.8 2.4 %collective-permute-start.25 = (bf16[128,1280]{1,0:T(8,128)(2,1)S(1)}, bf16[128,1280]{1,0:T(8,128)(2,1)S(1)}, u32[]{:S(2)}, u32[]{:S(2)}) collective-permute-start(bf16[128,1280]{1,0:T(8,128)(2,1)S(1)} %get-tuple-element.69), channel_id=1, source_target_pairs={{0,96},{32,64},{64,32},{96,0},{1,97},{33,65},{65,33},{97,1},{2,98}... | collective-permute-start | bytes 983048 | tf_op jit(solution)/shard_map/ppermute | solution.py:38
  113.2 0.9 collective-permute-start.26
  114.1 4.2 %collective-permute-done.27 = bf16[128,1280]{1,0:T(8,128)(2,1)S(1)} collective-permute-done((bf16[128,1280]{1,0:T(8,128)(2,1)S(1)}, bf16[128,1280]{1,0:T(8,128)(2,1)S(1)}, u32[]{:S(2)}, u32[]{:S(2)}) %collective-permute-start.27) | collective-permute-done | bytes 327712 | tf_op jit(solution)/shard_map/ppermute | solution.py:38
  118.2 0.1 add_convert_fusion
  118.3 0.1 collective-permute-start.28
  118.4 0.1 add_convert_fusion.1
  118.5 1.0 collective-permute-start.24
  119.6 5.7 %collective-permute-done.25.refs_3_ = bf16[128,1280]{1,0:T(8,128)(2,1)S(1)} collective-permute-done((bf16[128,1280]{1,0:T(8,128)(2,1)S(1)}, bf16[128,1280]{1,0:T(8,128)(2,1)S(1)}, u32[]{:S(2)}, u32[]{:S(2)}) %collective-permute-start.25) | collective-permute-done | bytes 327712 | tf_op jit(solution)/shard_map/ppermute | solution.py:38
  125.3 6.1 %collective-permute-done.28.refs_5_ = bf16[128,1280]{1,0:T(8,128)(2,1)S(1)} collective-permute-done((bf16[128,1280]{1,0:T(8,128)(2,1)S(1)}, bf16[128,1280]{1,0:T(8,128)(2,1)S(1)}, u32[]{:S(2)}, u32[]{:S(2)}) %collective-permute-start.28) | collective-permute-done | bytes 327712 | tf_op jit(solution)/shard_map/ppermute | solution.py:38
  131.4 0.9 collective-permute-done.24.refs_2_
  132.3 1.3 finish.1
  (67 shorter events, 0.4 us)
Async XLA Ops:
  3.0 5.6 %collective-permute-start = (bf16[128,640]{1,0:T(8,128)(2,1)}, bf16[128,640]{1,0:T(8,128)(2,1)S(1)}, u32[]{:S(2)}, u32[]{:S(2)}) collective-permute-start(bf16[128,640]{1,0:T(8,128)(2,1)} %get-tuple-element.40), channel_id=1, source_target_pairs={{0,32},{32,0},{64,96},{96,64},{1,33},{33,1},{65,97},{97,65},{2,34}... | collective-permute-start | bytes 491528 | tf_op jit(solution)/shard_map/ppermute | solution.py:38
  5.2 10.0 %collective-permute-start.1 = (bf16[128,640]{1,0:T(8,128)(2,1)}, bf16[128,640]{1,0:T(8,128)(2,1)S(1)}, u32[]{:S(2)}, u32[]{:S(2)}) collective-permute-start(bf16[128,640]{1,0:T(8,128)(2,1)} %get-tuple-element.41), channel_id=1, source_target_pairs={{0,64},{32,96},{64,0},{96,32},{1,65},{33,97},{65,1},{97,33},{2,66}... | collective-permute-start | bytes 491528 | tf_op jit(solution)/shard_map/ppermute | solution.py:38
  7.8 10.1 %collective-permute-start.2 = (bf16[128,640]{1,0:T(8,128)(2,1)}, bf16[128,640]{1,0:T(8,128)(2,1)S(1)}, u32[]{:S(2)}, u32[]{:S(2)}) collective-permute-start(bf16[128,640]{1,0:T(8,128)(2,1)} %get-tuple-element.42), channel_id=1, source_target_pairs={{0,96},{32,64},{64,32},{96,0},{1,97},{33,65},{65,33},{97,1},{2,98}... | collective-permute-start | bytes 491528 | tf_op jit(solution)/shard_map/ppermute | solution.py:38
  18.8 29.8 %copy-start.13 = (bf16[512,640]{1,0:T(8,128)(2,1)}, bf16[512,640]{1,0:T(8,128)(2,1)S(1)}, u32[]{:S(2)}) copy-start(bf16[512,640]{1,0:T(8,128)(2,1)S(1)} %slice_dynamic-update-slice_fusion.r_1_) | copy-start | bytes 1966084
  18.8 15.4 %collective-permute-start.9 = (bf16[512,640]{1,0:T(8,128)(2,1)S(1)}, bf16[512,640]{1,0:T(8,128)(2,1)S(1)}, u32[]{:S(2)}, u32[]{:S(2)}) collective-permute-start(bf16[512,640]{1,0:T(8,128)(2,1)S(1)} %slice_dynamic-update-slice_fusion.r_1_), channel_id=1, source_target_pairs={{0,1},{1,0},{2,3},{3,2},{4,5},{5,4},{6,7},{7,6},{8,9},{9,8},{10,11... | collective-permute-start | bytes 1966088 | tf_op jit(solution)/shard_map/ppermute | solution.py:46
  20.6 18.9 %collective-permute-start.3 = (bf16[512,640]{1,0:T(8,128)(2,1)S(1)}, bf16[512,640]{1,0:T(8,128)(2,1)S(1)}, u32[]{:S(2)}, u32[]{:S(2)}) collective-permute-start(bf16[512,640]{1,0:T(8,128)(2,1)S(1)} %slice_dynamic-update-slice_fusion.r_1_), channel_id=1, source_target_pairs={{0,7},{1,2},{2,1},{3,4},{4,3},{5,6},{6,5},{7,0},{8,15},{9,10},{10,... | collective-permute-start | bytes 1966088 | tf_op jit(solution)/shard_map/ppermute | solution.py:46
  27.5 11.9 %collective-permute-start.6 = (bf16[64,640]{1,0:T(8,128)(2,1)}, bf16[64,640]{1,0:T(8,128)(2,1)S(1)}, u32[]{:S(2)}, u32[]{:S(2)}) collective-permute-start(bf16[64,640]{1,0:T(8,128)(2,1)} %get-tuple-element.46), channel_id=1, source_target_pairs={{0,32},{32,0},{64,96},{96,64},{1,33},{33,1},{65,97},{97,65},{2,34}... | collective-permute-start | bytes 245768 | tf_op jit(solution)/shard_map/ppermute | solution.py:38
  27.5 12.0 %collective-permute-start.7 = (bf16[64,640]{1,0:T(8,128)(2,1)}, bf16[64,640]{1,0:T(8,128)(2,1)S(1)}, u32[]{:S(2)}, u32[]{:S(2)}) collective-permute-start(bf16[64,640]{1,0:T(8,128)(2,1)} %get-tuple-element.47), channel_id=1, source_target_pairs={{0,64},{32,96},{64,0},{96,32},{1,65},{33,97},{65,1},{97,33},{2,66}... | collective-permute-start | bytes 245768 | tf_op jit(solution)/shard_map/ppermute | solution.py:38
  28.7 10.8 %collective-permute-start.8 = (bf16[64,640]{1,0:T(8,128)(2,1)}, bf16[64,640]{1,0:T(8,128)(2,1)S(1)}, u32[]{:S(2)}, u32[]{:S(2)}) collective-permute-start(bf16[64,640]{1,0:T(8,128)(2,1)} %get-tuple-element.48), channel_id=1, source_target_pairs={{0,96},{32,64},{64,32},{96,0},{1,97},{33,65},{65,33},{97,1},{2,98}... | collective-permute-start | bytes 245768 | tf_op jit(solution)/shard_map/ppermute | solution.py:38
  34.2 17.1 %copy-start.7 = (bf16[512,640]{1,0:T(8,128)(2,1)}, bf16[512,640]{1,0:T(8,128)(2,1)S(1)}, u32[]{:S(2)}) copy-start(bf16[512,640]{1,0:T(8,128)(2,1)S(1)} %collective-permute-done.9.r_1_) | copy-start | bytes 1966084
  34.2 20.6 %collective-permute-start.15 = (bf16[512,640]{1,0:T(8,128)(2,1)S(1)}, bf16[512,640]{1,0:T(8,128)(2,1)S(1)}, u32[]{:S(2)}, u32[]{:S(2)}) collective-permute-start(bf16[512,640]{1,0:T(8,128)(2,1)S(1)} %collective-permute-done.9.r_1_), channel_id=1, source_target_pairs={{0,7},{1,2},{2,1},{3,4},{4,3},{5,6},{6,5},{7,0},{8,15},{9,10},{10,... | collective-permute-start | bytes 1966088 | tf_op jit(solution)/shard_map/ppermute | solution.py:46
  39.4 11.9 %copy-start.9 = (bf16[512,640]{1,0:T(8,128)(2,1)}, bf16[512,640]{1,0:T(8,128)(2,1)S(1)}, u32[]{:S(2)}) copy-start(bf16[512,640]{1,0:T(8,128)(2,1)S(1)} %collective-permute-done.3.r_2_) | copy-start | bytes 1966084
  39.4 13.7 %collective-permute-start.4 = (bf16[512,640]{1,0:T(8,128)(2,1)S(1)}, bf16[512,640]{1,0:T(8,128)(2,1)S(1)}, u32[]{:S(2)}, u32[]{:S(2)}) collective-permute-start(bf16[512,640]{1,0:T(8,128)(2,1)S(1)} %collective-permute-done.3.r_2_), channel_id=1, source_target_pairs={{0,1},{1,0},{2,3},{3,2},{4,5},{5,4},{6,7},{7,6},{8,9},{9,8},{10,11... | collective-permute-start | bytes 1966088 | tf_op jit(solution)/shard_map/ppermute | solution.py:46
  40.5 8.0 %collective-permute-start.11 = (bf16[256,640]{1,0:T(8,128)(2,1)S(1)}, bf16[256,640]{1,0:T(8,128)(2,1)S(1)}, u32[]{:S(2)}, u32[]{:S(2)}) collective-permute-start(bf16[256,640]{1,0:T(8,128)(2,1)S(1)} %pad_maximum_fusion), channel_id=1, source_target_pairs={{0,24},{8,16},{16,8},{24,0},{1,25},{9,17},{17,9},{25,1},{2,26},{10... | collective-permute-start | bytes 983048 | tf_op jit(solution)/shard_map/ppermute | solution.py:42
  43.9 6.4 %collective-permute-start.10 = (bf16[256,640]{1,0:T(8,128)(2,1)S(1)}, bf16[256,640]{1,0:T(8,128)(2,1)S(1)}, u32[]{:S(2)}, u32[]{:S(2)}) collective-permute-start(bf16[256,640]{1,0:T(8,128)(2,1)S(1)} %pad_maximum_fusion), channel_id=1, source_target_pairs={{0,8},{8,0},{16,24},{24,16},{1,9},{9,1},{17,25},{25,17},{2,10},{10... | collective-permute-start | bytes 983048 | tf_op jit(solution)/shard_map/ppermute | solution.py:42
  48.5 6.4 %collective-permute-start.12 = (bf16[128,640]{1,0:T(8,128)(2,1)S(1)}, bf16[128,640]{1,0:T(8,128)(2,1)S(1)}, u32[]{:S(2)}, u32[]{:S(2)}) collective-permute-start(bf16[128,640]{1,0:T(8,128)(2,1)S(1)} %slice.54), channel_id=1, source_target_pairs={{0,8},{8,0},{16,24},{24,16},{1,9},{9,1},{17,25},{25,17},{2,10},{10... | collective-permute-start | bytes 491528 | tf_op jit(solution)/shard_map/ppermute | solution.py:42
  50.4 5.6 %copy-start.14 = (bf16[512,640]{1,0:T(8,128)(2,1)S(1)}, bf16[512,640]{1,0:T(8,128)(2,1)}, u32[]{:S(2)}) copy-start(bf16[512,640]{1,0:T(8,128)(2,1)} %copy-done.13) | copy-start | bytes 1966084
  50.4 5.5 %collective-permute-start.13 = (bf16[128,640]{1,0:T(8,128)(2,1)S(1)}, bf16[128,640]{1,0:T(8,128)(2,1)S(1)}, u32[]{:S(2)}, u32[]{:S(2)}) collective-permute-start(bf16[128,640]{1,0:T(8,128)(2,1)S(1)} %slice.55), channel_id=1, source_target_pairs={{0,24},{8,16},{16,8},{24,0},{1,25},{9,17},{17,9},{25,1},{2,26},{10... | collective-permute-start | bytes 491528 | tf_op jit(solution)/shard_map/ppermute | solution.py:42
  53.1 17.3 %collective-permute-start.14 = (bf16[512,640]{1,0:T(8,128)(2,1)S(1)}, bf16[512,640]{1,0:T(8,128)(2,1)S(1)}, u32[]{:S(2)}, u32[]{:S(2)}) collective-permute-start(bf16[512,640]{1,0:T(8,128)(2,1)S(1)} %collective-permute-done.4.r_1_), channel_id=1, source_target_pairs={{0,7},{1,2},{2,1},{3,4},{4,3},{5,6},{6,5},{7,0},{8,15},{9,10},{10,... | collective-permute-start | bytes 1966088 | tf_op jit(solution)/shard_map/ppermute | solution.py:46
  54.8 16.5 %collective-permute-start.16 = (bf16[512,640]{1,0:T(8,128)(2,1)S(1)}, bf16[512,640]{1,0:T(8,128)(2,1)S(1)}, u32[]{:S(2)}, u32[]{:S(2)}) collective-permute-start(bf16[512,640]{1,0:T(8,128)(2,1)S(1)} %collective-permute-done.15.r_2_), channel_id=1, source_target_pairs={{0,1},{1,0},{2,3},{3,2},{4,5},{5,4},{6,7},{7,6},{8,9},{9,8},{10,11... | collective-permute-start | bytes 1966088 | tf_op jit(solution)/shard_map/ppermute | solution.py:46
  55.9 8.9 %copy-start = (bf16[1024,640]{1,0:T(8,128)(2,1)}, bf16[1024,640]{1,0:T(8,128)(2,1)S(1)}, u32[]{:S(2)}) copy-start(bf16[1024,640]{1,0:T(8,128)(2,1)S(1)} %constant_dynamic-update-slice_fusion.r_0_) | copy-start | bytes 3932164
  55.9 3.3 %copy-start.8 = (bf16[512,640]{1,0:T(8,128)(2,1)S(1)}, bf16[512,640]{1,0:T(8,128)(2,1)}, u32[]{:S(2)}) copy-start(bf16[512,640]{1,0:T(8,128)(2,1)} %copy-done.7) | copy-start | bytes 1966084
  56.0 3.3 %copy-start.10 = (bf16[512,640]{1,0:T(8,128)(2,1)S(1)}, bf16[512,640]{1,0:T(8,128)(2,1)}, u32[]{:S(2)}) copy-start(bf16[512,640]{1,0:T(8,128)(2,1)} %copy-done.9) | copy-start | bytes 1966084
  70.5 1.7 %copy-start.2 = (bf16[512,640]{1,0:T(8,128)(2,1)}, bf16[512,640]{1,0:T(8,128)(2,1)S(1)}, u32[]{:S(2)}) copy-start(bf16[512,640]{1,0:T(8,128)(2,1)S(1)} %collective-permute-done.14.r_2_) | copy-start | bytes 1966084
  71.3 0.9 copy-start.4
  72.2 11.9 %collective-permute-start.17 = (bf16[256,640]{1,0:T(8,128)(2,1)}, bf16[256,640]{1,0:T(8,128)(2,1)S(1)}, u32[]{:S(2)}, u32[]{:S(2)}) collective-permute-start(bf16[256,640]{1,0:T(8,128)(2,1)} %slice.56), channel_id=1, source_target_pairs={{0,1},{1,0},{2,3},{3,2},{4,5},{5,4},{6,7},{7,6},{8,9},{9,8},{10,11... | collective-permute-start | bytes 983048 | tf_op jit(solution)/shard_map/ppermute | solution.py:46
  73.4 10.8 %collective-permute-start.18 = (bf16[256,640]{1,0:T(8,128)(2,1)}, bf16[256,640]{1,0:T(8,128)(2,1)S(1)}, u32[]{:S(2)}, u32[]{:S(2)}) collective-permute-start(bf16[256,640]{1,0:T(8,128)(2,1)} %slice.57), channel_id=1, source_target_pairs={{0,7},{1,2},{2,1},{3,4},{4,3},{5,6},{6,5},{7,0},{8,15},{9,10},{10,... | collective-permute-start | bytes 983048 | tf_op jit(solution)/shard_map/ppermute | solution.py:46
  75.0 1.3 copy-start.1
  76.4 1.1 copy-start.3
  77.5 1.1 copy-start.5
  84.2 22.7 %slice-start = ((s8[6553600]{0:T(1024)(128)(4,1)}), s8[4194304]{0:T(1024)(128)(4,1)S(1)}, s32[]{:S(2)}) async-start(s8[6553600]{0:T(1024)(128)(4,1)} %bitcast.5), calls=%async_computation | async-start | bytes 8388608
  84.9 5.2 %copy-start.6 = (bf16[1,64,5120]{2,1,0:T(8,128)(2,1)S(1)}, bf16[1,64,5120]{2,1,0:T(8,128)(2,1)}, u32[]{:S(2)}) copy-start(bf16[1,64,5120]{2,1,0:T(8,128)(2,1)} %own_ref.1) | copy-start | bytes 1966084
  85.0 21.9 %slice-start.1 = ((s8[6553600]{0:T(1024)(128)(4,1)}), s8[2359296]{0:T(1024)(128)(4,1)S(1)}, s32[]{:S(2)}) async-start(s8[6553600]{0:T(1024)(128)(4,1)} %bitcast.5), calls=%async_computation.1 | async-start | bytes 4718592
  85.0 14.3 %collective-permute-start.20 = (bf16[656,256]{1,0:T(8,128)(2,1)S(1)}, bf16[656,256]{1,0:T(8,128)(2,1)S(1)}, u32[]{:S(2)}, u32[]{:S(2)}) collective-permute-start(bf16[656,256]{1,0:T(8,128)(2,1)S(1)} %attend_last.3), channel_id=1, source_target_pairs={{0,16},{8,24},{16,0},{24,8},{1,17},{9,25},{17,1},{25,9},{2,18},{10... | collective-permute-start | bytes 1007624 | tf_op jit(solution)/shard_map/ppermute | solution.py:42
  88.3 11.0 %collective-permute-start.19 = (bf16[656,256]{1,0:T(8,128)(2,1)S(1)}, bf16[656,256]{1,0:T(8,128)(2,1)S(1)}, u32[]{:S(2)}, u32[]{:S(2)}) collective-permute-start(bf16[656,256]{1,0:T(8,128)(2,1)S(1)} %get-tuple-element.61), channel_id=1, source_target_pairs={{0,8},{8,0},{16,24},{24,16},{1,9},{9,1},{17,25},{25,17},{2,10},{10... | collective-permute-start | bytes 1007624 | tf_op jit(solution)/shard_map/ppermute | solution.py:42
  88.6 10.6 %collective-permute-start.21 = (bf16[656,256]{1,0:T(8,128)(2,1)S(1)}, bf16[656,256]{1,0:T(8,128)(2,1)S(1)}, u32[]{:S(2)}, u32[]{:S(2)}) collective-permute-start(bf16[656,256]{1,0:T(8,128)(2,1)S(1)} %get-tuple-element.63), channel_id=1, source_target_pairs={{0,24},{8,16},{16,8},{24,0},{1,25},{9,17},{17,9},{25,1},{2,26},{10... | collective-permute-start | bytes 1007624 | tf_op jit(solution)/shard_map/ppermute | solution.py:42
  90.2 9.9 %collective-permute-start.5 = (bf16[64,2560]{1,0:T(8,128)(2,1)S(1)}, bf16[64,2560]{1,0:T(8,128)(2,1)S(1)}, u32[]{:S(2)}, u32[]{:S(2)}) collective-permute-start(bf16[64,2560]{1,0:T(8,128)(2,1)S(1)} %dynamic-slice_bitcast_fusion), channel_id=1, source_target_pairs={{0,128},{128,0},{1,129},{129,1},{2,130},{130,2},{3,131},{131,3},{4... | collective-permute-start | bytes 983048 | tf_op jit(solution)/shard_map/ppermute | solution.py:50
  100.1 6.7 %collective-permute-start.22 = (bf16[256,640]{1,0:T(8,128)(2,1)S(1)}, bf16[256,640]{1,0:T(8,128)(2,1)S(1)}, u32[]{:S(2)}, u32[]{:S(2)}) collective-permute-start(bf16[256,640]{1,0:T(8,128)(2,1)S(1)} %join.1.r_1_), channel_id=1, source_target_pairs={{0,128},{128,0},{1,129},{129,1},{2,130},{130,2},{3,131},{131,3},{4... | collective-permute-start | bytes 983048 | tf_op jit(solution)/shard_map/ppermute | solution.py:50
  108.0 10.2 %collective-permute-start.27 = (bf16[128,1280]{1,0:T(8,128)(2,1)S(1)}, bf16[128,1280]{1,0:T(8,128)(2,1)S(1)}, u32[]{:S(2)}, u32[]{:S(2)}) collective-permute-start(bf16[128,1280]{1,0:T(8,128)(2,1)S(1)} %get-tuple-element.72), channel_id=1, source_target_pairs={{0,96},{32,64},{64,32},{96,0},{1,97},{33,65},{65,33},{97,1},{2,98}... | collective-permute-start | bytes 983048 | tf_op jit(solution)/shard_map/ppermute | solution.py:38
  108.1 10.3 %collective-permute-start.23 = (bf16[128,1280]{1,0:T(8,128)(2,1)S(1)}, bf16[128,1280]{1,0:T(8,128)(2,1)S(1)}, u32[]{:S(2)}, u32[]{:S(2)}) collective-permute-start(bf16[128,1280]{1,0:T(8,128)(2,1)S(1)} %get-tuple-element.68), channel_id=1, source_target_pairs={{0,32},{32,0},{64,96},{96,64},{1,33},{33,1},{65,97},{97,65},{2,34}... | collective-permute-start | bytes 983048 | tf_op jit(solution)/shard_map/ppermute | solution.py:38
  110.8 21.5 %copy-start.11 = (f32[5120]{0:T(1024)S(1)}, f32[5120]{0:T(1024)}, u32[]{:S(2)}) copy-start(f32[5120]{0:T(1024)} %gate_ref.1) | copy-start | bytes 61444
  110.8 21.5 %copy-start.12 = (f32[5120]{0:T(1024)S(1)}, f32[5120]{0:T(1024)}, u32[]{:S(2)}) copy-start(f32[5120]{0:T(1024)} %bias_ref.1) | copy-start | bytes 61444
  110.8 14.4 %collective-permute-start.25 = (bf16[128,1280]{1,0:T(8,128)(2,1)S(1)}, bf16[128,1280]{1,0:T(8,128)(2,1)S(1)}, u32[]{:S(2)}, u32[]{:S(2)}) collective-permute-start(bf16[128,1280]{1,0:T(8,128)(2,1)S(1)} %get-tuple-element.69), channel_id=1, source_target_pairs={{0,96},{32,64},{64,32},{96,0},{1,97},{33,65},{65,33},{97,1},{2,98}... | collective-permute-start | bytes 983048 | tf_op jit(solution)/shard_map/ppermute | solution.py:38
  113.2 12.0 %collective-permute-start.26 = (bf16[128,1280]{1,0:T(8,128)(2,1)S(1)}, bf16[128,1280]{1,0:T(8,128)(2,1)S(1)}, u32[]{:S(2)}, u32[]{:S(2)}) collective-permute-start(bf16[128,1280]{1,0:T(8,128)(2,1)S(1)} %get-tuple-element.70), channel_id=1, source_target_pairs={{0,32},{32,0},{64,96},{96,64},{1,33},{33,1},{65,97},{97,65},{2,34}... | collective-permute-start | bytes 983048 | tf_op jit(solution)/shard_map/ppermute | solution.py:38
  118.3 13.1 %collective-permute-start.28 = (bf16[128,1280]{1,0:T(8,128)(2,1)S(1)}, bf16[128,1280]{1,0:T(8,128)(2,1)S(1)}, u32[]{:S(2)}, u32[]{:S(2)}) collective-permute-start(bf16[128,1280]{1,0:T(8,128)(2,1)S(1)} %add_convert_fusion), channel_id=1, source_target_pairs={{0,32},{32,0},{64,96},{96,64},{1,33},{33,1},{65,97},{97,65},{2,34}... | collective-permute-start | bytes 983048 | tf_op jit(solution)/shard_map/ppermute | solution.py:38
  118.5 13.8 %collective-permute-start.24 = (bf16[128,1280]{1,0:T(8,128)(2,1)S(1)}, bf16[128,1280]{1,0:T(8,128)(2,1)S(1)}, u32[]{:S(2)}, u32[]{:S(2)}) collective-permute-start(bf16[128,1280]{1,0:T(8,128)(2,1)S(1)} %add_convert_fusion.1), channel_id=1, source_target_pairs={{0,96},{32,64},{64,32},{96,0},{1,97},{33,65},{65,33},{97,1},{2,98}... | collective-permute-start | bytes 983048 | tf_op jit(solution)/shard_map/ppermute | solution.py:38
